TPU v7x, 128 devices: a whole 4x4x4 slice. The times are simulated.
128 devices in a mesh: ctx: 64 (over x, z_lo, y, core), fsdp: 2 (over z_hi).
Axes of the slice: x: 4, y: 4, z: 4 (z_hi: 2, z_lo: 2; z = z_hi * 2 + z_lo), core: 2. Of those that a mesh axis runs over, the one named last changes fastest.
Arguments:
- hidden_in: bfloat16 [2, 8192, 768], P('fsdp', 'ctx'), may hold values from -6 to 6
- doc_lengths: int32 [2, 2, 8], P('fsdp'), may hold values from 1 to 2048, as said below
- norm_gain: bfloat16 [2, 2, 768], P(None, None, 'fsdp'), may hold values from 0.25 to 1.75
- norm_bias: bfloat16 [2, 2, 768], P(None, None, 'fsdp'), may hold values from -1.796875 to 1.796875
- qkv_weight: bfloat16 [2, 768, 2304], P(None, 'fsdp'), may hold values from -0.21875 to 0.21875
- qkv_bias: bfloat16 [2, 2304], P(None, 'fsdp'), may hold values from -3 to 3
- out_weight: bfloat16 [2, 768, 768], P(None, 'fsdp'), may hold values from -0.875 to 0.875
- out_bias: bfloat16 [2, 768], P(None, 'fsdp'), may hold values from -3 to 3
- up_weight: bfloat16 [2, 768, 3072], P(None, 'fsdp'), may hold values from -0.21875 to 0.21875
- up_bias: bfloat16 [2, 3072], P(None, 'fsdp'), may hold values from -3 to 3
- down_weight: bfloat16 [2, 3072, 768], P(None, 'fsdp'), may hold values from -0.109375 to 0.109375
- down_bias: bfloat16 [2, 768], P(None, 'fsdp'), may hold values from -3 to 3
- cotangent: bfloat16 [2, 8192, 768], P('fsdp', 'ctx'), may hold values from -6 to 6
Outputs:
- hidden_out: bfloat16 [2, 8192, 768], P('fsdp', 'ctx')
- hidden_grad: float32 [2, 8192, 768], P('fsdp', 'ctx')
- norm_gain_grad: float32 [2, 2, 768], P(None, None, 'fsdp')
- norm_bias_grad: float32 [2, 2, 768], P(None, None, 'fsdp')
- qkv_weight_grad: float32 [2, 768, 2304], P(None, 'fsdp')
- qkv_bias_grad: float32 [2, 2304], P(None, 'fsdp')
- out_weight_grad: float32 [2, 768, 768], P(None, 'fsdp')
- out_bias_grad: float32 [2, 768], P(None, 'fsdp')
- up_weight_grad: float32 [2, 768, 3072], P(None, 'fsdp')
- up_bias_grad: float32 [2, 3072], P(None, 'fsdp')
- down_weight_grad: float32 [2, 3072, 768], P(None, 'fsdp')
- down_bias_grad: float32 [2, 768], P(None, 'fsdp')
Inputs may be any that keep to these rules, and one draw needn't show every extreme that they name: `doc_lengths`: row [g, s] holds the lengths of the 8 documents that fill sequence s of group g, in order; they sum to 4096, the last is end padding of 1 to 32 tokens, and the one before it is 2048 long, the largest of the row.
All inputs are finite; a program needn't handle non-finite values.
Results may differ from a plain program's by a relative error of at most 0.013.
Values may be sent and summed in bfloat16 or wider, within the bound.
No kernel may reach another device: no remote copies, remote signals or barrier semaphores. Data moves between devices by JAX's collectives and lax.ppermute only.
A program may use at most 384 MiB of HBM per device.

v0:
```python
import functools

import jax
import jax.numpy as jnp
from jax import lax
from jax.experimental import pallas as pl
from jax.experimental.pallas import tpu as pltpu
from jax.sharding import Mesh
from jax.sharding import PartitionSpec as P

D = 768
HALF = D // 2
HEADS = 12
HEAD = 64
FF = 3072
ROT = 16
LAYERS = 2
WINDOW = 1024
DOCS = 8
TILE = 128
TILES = 16
UNIT = TILE * TILES
SLOTS = 8
CORE_HEADS = HEADS // 2
QKV = 3 * HEAD
QKV_ROWS = CORE_HEADS * QKV
CORE_FF = FF // 2
QUARTER = FF // 4

CHUNK_UP = 96
CHUNK_DOWN = 48
CHUNK = CHUNK_UP + 2 * CHUNK_DOWN
QKV_PART = QKV_ROWS // 4
OUT_PART = QKV // 2
PART_SECOND = 2 * HALF
PART_FIRST = 2 * HALF + OUT_PART + 32
PART_QKV = QKV_PART + OUT_PART
CHUNK_SECOND, CHUNK_FIRST, CHUNK_QKV = PART_SECOND // 4, PART_FIRST // 4, PART_QKV // 4
SENT_GATE, SENT_CTX = HALF, HALF + QUARTER
SENT_EARLY = SENT_CTX + QKV + HEAD
SENT_LATE = CORE_FF + D
QKV_FIRST = 32 * 40
SMALL = 12

BLOCKED = -1e30
EPSILON = 1e-05
SWAP = [(0, 1), (1, 0)]
F32 = jnp.float32
BF16 = jnp.bfloat16

NN = (((1,), (0,)), ((), ()))
NT = (((1,), (1,)), ((), ()))
TN = (((0,), (0,)), ((), ()))


def dot(left, right, dims=NN):
    return lax.dot_general(left, right, dims, preferred_element_type=F32)


def shape(dims, kind):
    return jax.ShapeDtypeStruct(dims, kind)


def block(dims, *at):
    place = at[0] if at else (lambda s: (0,) * len(dims))
    return pl.BlockSpec(dims, lambda i, s: place(s))


def whole(array):
    return block(array.shape)


LATEST = []


def run(
    kernel, scalars, inputs, outs, name, flops, moved, scratch=(), limit=40, aliases=None, exps=0, out_specs=None, after=(), token=False
):
    after = list(after) + LATEST
    arrays = [item[0] if isinstance(item, tuple) else item for item in inputs] + after
    specs = [item[1] if isinstance(item, tuple) else whole(item) for item in inputs]
    specs += [pl.BlockSpec(memory_space=pl.ANY)] * len(after)
    if out_specs is None:
        out_specs = [block(out.shape) for out in outs]
    count = len(inputs)

    def body(at, *refs):
        kernel(at, *refs[:count], *refs[count + len(after) :])

    results = pl.pallas_call(
        body,
        grid_spec=pltpu.PrefetchScalarGridSpec(
            num_scalar_prefetch=1,
            grid=(1,),
            in_specs=specs,
            out_specs=out_specs,
            scratch_shapes=list(scratch),
        ),
        out_shape=outs,
        input_output_aliases=aliases or {},
        compiler_params=pltpu.CompilerParams(vmem_limit_bytes=60 * 1024 * 1024),
        cost_estimate=pl.CostEstimate(flops=1, bytes_accessed=1, transcendentals=0),
        name=name,
    )(scalars, *arrays)
    LATEST[:] = [results[-1] if token else min(results, key=lambda result: result.size)]
    return results


def held(at, values, after=()):
    anywhere = pl.BlockSpec(memory_space=pl.ANY)

    def kernel(at, *refs):
        refs[-1][...] = jnp.zeros_like(refs[-1])

    outs = [shape(value.shape, value.dtype) for value in values] + [shape((8, 128), F32)]
    specs = [anywhere] * len(values) + [block((8, 128))]
    aliases = {1 + index: index for index in range(len(values))}
    inputs = [(value, anywhere) for value in values]
    return run(kernel, at, inputs, outs, "held", 0, 0, aliases=aliases, out_specs=specs, after=after, token=True)[:-1]


CORE, ZH, REVERSE, SWAPPED, FIRST_HALF, LAST_CHIP, RING_X, RING_Y, SPOT = range(9)


def half_at(index):
    return pl.ds(pl.multiple_of(index * HALF, HALF), HALF)


def turn(at, raw_ref, out_ref):
    def by_core(core):
        for part in range(3):
            for z in range(2):
                start = part * D + z * HALF + core * QKV
                piece = raw_ref[0, :, start : start + QKV].T
                for head in range(3):
                    row = (z * 3 + head) * QKV + part * HEAD
                    out_ref[row : row + HEAD, :] = piece[head * HEAD : (head + 1) * HEAD]

    for core in range(2):
        pl.when(at[CORE] == core)(functools.partial(by_core, core))


def put_chunk(up_ref, down_ref, out_ref):
    out_ref[0:CHUNK_UP] = up_ref[0]
    out_ref[CHUNK_UP : CHUNK_UP + CHUNK_DOWN] = down_ref[0, :, :HALF]
    out_ref[CHUNK_UP + CHUNK_DOWN :] = down_ref[0, :, HALF:]


SMALL_AT, CHUNK_AT = QKV_ROWS, QKV_ROWS + 32


def begin_kernel(at, qkv_ref, up_ref, down_ref, *refs):
    small, out_ref = refs[:-1], refs[-1]
    turn(at, qkv_ref, out_ref)
    out_ref[SMALL_AT:CHUNK_AT] = gather_small(small).astype(BF16)
    put_chunk(up_ref, down_ref, out_ref.at[CHUNK_AT:])


def begin(at, qkv_weight, up_weight, down_weight, small):
    return run(
        begin_kernel,
        at,
        [
            (qkv_weight, block((1, HALF, 3 * D), lambda s: (0, 0, 0))),
            *chunk_inputs(up_weight, down_weight, 0),
            *small,
        ],
        [shape((CHUNK_AT + CHUNK, HALF), BF16)],
        "begin",
        0,
        2700000,
    )[0]


def chunk_inputs(up_weight, down_weight, layer):
    column = lambda s: (s[RING_Y] // 2) * 4 + s[CORE] * 2 + s[RING_Y] % 2
    return [
        (up_weight, block((1, CHUNK_UP, HALF), lambda s: (layer, s[RING_X], column(s)))),
        (down_weight, block((1, CHUNK_DOWN, D), lambda s: (layer, s[CORE] * 16 + s[SPOT], 0))),
    ]


REST_CHUNK = LAYERS * HALF


def begin_rest_kernel(at, qkv_ref, up_ref, down_ref, out_ref, rows_ref, turned_ref):
    for layer in range(LAYERS):
        for side in range(2):
            row = layer * HALF + side * QKV
            rows_ref[row : row + QKV] = out_ref[layer, :, side * HALF : (side + 1) * HALF]
    put_chunk(up_ref, down_ref, rows_ref.at[REST_CHUNK:])
    turn(at, qkv_ref, turned_ref)


def begin_rest(at, qkv_weight, up_weight, down_weight, out_weight):
    return run(
        begin_rest_kernel,
        at,
        [
            (qkv_weight, block((1, HALF, 3 * D), lambda s: (1, 0, 0))),
            *chunk_inputs(up_weight, down_weight, 1),
            (out_weight, block((LAYERS, QKV, D), lambda s: (0, s[CORE], 0))),
        ],
        [shape((REST_CHUNK + CHUNK, HALF), BF16), shape((QKV_ROWS, HALF), BF16)],
        "begin_rest",
        0,
        1500000,
    )


def fill_up(z, up_ref, own0_ref, own1_ref, rest_ref):
    up_ref[half_at(z), 0:QUARTER] = own0_ref[0]
    up_ref[half_at(z), QUARTER:] = own1_ref[0]
    for chunk in range(16):
        x, y = chunk // 4, chunk % 4
        rows = pl.ds(pl.multiple_of((1 - z) * HALF + CHUNK_UP * x, 32), CHUNK_UP)
        up_ref[rows, y * HALF : (y + 1) * HALF] = rest_ref[chunk]


def fill_down(z, down_ref, own_ref, rest_ref):
    down_ref[pl.ds(pl.multiple_of(z * QUARTER, QUARTER), QUARTER), :] = own_ref[0]
    for chunk in range(16):
        rows = pl.ds(pl.multiple_of((1 - z) * QUARTER + CHUNK_DOWN * chunk, 16), CHUNK_DOWN)
        down_ref[rows, 0:HALF] = rest_ref[chunk, 0:CHUNK_DOWN]
        down_ref[rows, HALF:] = rest_ref[chunk, CHUNK_DOWN:]


def fill_out(z, out_ref, own_ref, other_ref):
    out_ref[pl.ds(pl.multiple_of(z * QKV, QKV), QKV), :] = own_ref[0]
    for side in range(2):
        rows = slice(side * QKV, (side + 1) * QKV)
        out_ref[pl.ds(pl.multiple_of((1 - z) * QKV, QKV), QKV), side * HALF : (side + 1) * HALF] = other_ref[rows, :]


def up_inputs(weights, rest, layer):
    own = [
        (weights, block((1, HALF, QUARTER), lambda s, z=z: (layer, 0, 2 * z + s[CORE]))) for z in range(2)
    ]
    return own + [(rest[layer], block((16, CHUNK_UP, HALF), lambda s: (0, 0, 0)))]


def down_inputs(weights, rest, layer):
    return [
        (weights, block((1, QUARTER, D), lambda s: (layer, s[CORE], 0))),
        (rest[layer], block((16, 2 * CHUNK_DOWN, HALF), lambda s: (0, 1, 0))),
    ]


def out_inputs(own, other, layer):
    return [
        (own, block((1, QKV, D), lambda s: (layer, s[CORE], 0))),
        (other, block((HALF, HALF), lambda s: (layer, 0))),
    ]


def norm_kernel(at, *refs, first):
    if first:
        stream_ref, gain_ref, offset_ref, hat_ref, inverse_ref, act_ref = refs
        stream = stream_ref[...].astype(F32)
    else:
        stream_ref, keep_ref, got_ref, bias_ref, gain_ref, offset_ref, next_ref, hat_ref, inverse_ref, act_ref = refs
        stream = stream_ref[...].astype(F32) + (keep_ref[...] + got_ref[...] + bias_ref[...])
        next_ref[...] = stream
    centered = stream - jnp.mean(stream, axis=-1, keepdims=True)
    inverse = lax.rsqrt(jnp.mean(centered * centered, axis=-1, keepdims=True) + EPSILON)
    hat = centered * inverse
    hat_ref[...] = hat
    inverse_ref[...] = inverse
    act_ref[:, 0:D] = (hat * gain_ref[0:1] + offset_ref[0:1]).astype(BF16)
    act_ref[:, D:] = (hat * gain_ref[1:2] + offset_ref[1:2]).astype(BF16)


def norms(at, stream, added, gain, offset):
    outs = [shape((TILE, D), F32), shape((TILE, 1), F32), shape((TILE, 2 * D), BF16)]
    if added is None:
        kernel = functools.partial(norm_kernel, first=True)
        return [None, *run(kernel, at, [stream, gain, offset], outs, "norms", 1000000, 1200000)]
    kernel = functools.partial(norm_kernel, first=False)
    outs = [shape((TILE, D), F32)] + outs
    return run(kernel, at, [stream, *added, gain, offset], outs, "norms", 1000000, 2400000)


def assemble(target_ref, mine, theirs):
    rows = TILE // 2
    target_ref[0:rows] = mine[:rows]
    target_ref[rows : 2 * rows] = theirs[:rows]
    target_ref[2 * rows : 3 * rows] = mine[rows:]
    target_ref[3 * rows :] = theirs[rows:]


def qkv_kernel(at, mine_ref, theirs_ref, own_ref, other_ref, bias_ref, cos_ref, sin_ref, *refs):
    along, (out_ref, tok_ref, act_t) = refs[:-3], refs[-3:]
    z = at[ZH]
    assemble(tok_ref, mine_ref[...], theirs_ref[...])
    act_t[...] = tok_ref[...].T
    cosine, sine = cos_ref[...], sin_ref[...]

    def rotated(part):
        low, high = part[:8], part[8:ROT]
        return jnp.concatenate(
            [low * cosine - high * sine, high * cosine + low * sine, part[ROT:]], axis=0
        )

    own_act, other_act = act_t[half_at(z), :], act_t[half_at(1 - z), :]
    for head in range(CORE_HEADS):
        rows = slice(head * QKV, (head + 1) * QKV)
        value = dot(own_ref[rows, :], own_act) + dot(other_ref[rows, :], other_act)
        bias = jnp.broadcast_to(bias_ref[head : head + 1, :], (8, QKV)).T
        value = value + bias[:, 0:1]
        query = (rotated(value[:HEAD]).astype(BF16).astype(F32) * 0.125).astype(BF16)
        key = rotated(value[HEAD : 2 * HEAD]).astype(BF16)
        val = value[2 * HEAD :].astype(BF16)
        for seq in range(2):
            lanes = slice(seq * TILE, (seq + 1) * TILE)
            out_ref[seq, head, 0:HEAD, :] = query[:, lanes]
            out_ref[seq, head, HEAD : 2 * HEAD, :] = key[:, lanes]
            out_ref[seq, head, 2 * HEAD : QKV, :] = val[:, lanes]
    for seq in range(2):
        out_ref[seq, CORE_HEADS:, 0:QKV, :] = jnp.zeros((SLOTS - CORE_HEADS, QKV, TILE), BF16)
        if along:
            out_ref[seq, :, QKV:, :] = along[0][seq * SLOTS : (seq + 1) * SLOTS]


def turned(weights):
    return weights, block((QKV_ROWS, HALF), lambda s: (0, 0))


def project_qkv(at, mine, theirs, own, other, bias, cosine, sine, along=None):
    left = block((TILE, D), lambda s: (0, 0))
    return run(
        qkv_kernel,
        at,
        [(mine, left), (theirs, left), turned(own), turned(other), bias, cosine, sine]
        + ([] if along is None else [along]),
        [shape((2, SLOTS, QKV if along is None else QKV + HEAD, TILE), BF16)],
        "qkv",
        4 * TILE * D * QKV_ROWS,
        3500000,
        [pltpu.VMEM((2 * TILE, D), BF16), pltpu.VMEM((D, 2 * TILE), BF16)],
        limit=24,
    )[0]


def mlp_kernel(
    at, mine_ref, theirs_ref, bias_ref, up0_ref, up1_ref, up_rest, down_own, down_rest, gate_ref, slope_ref, sum_ref, act, up, down
):
    z = at[ZH]
    act[0:TILE] = mine_ref[...]
    act[TILE:] = theirs_ref[...]
    fill_up(z, up, up0_ref, up1_ref, up_rest)
    fill_down(z, down, down_own, down_rest)
    total = jnp.zeros((2 * TILE, D), F32)
    for part in range(4):
        lanes = slice(part * HALF, (part + 1) * HALF)
        value = dot(act[...], up[:, lanes]) + bias_ref[:, lanes]
        normal = 0.5 * (1.0 + lax.erf(value * 0.7071067811865476))
        gate = (value * normal).astype(BF16)
        gate_ref[:, lanes] = gate
        slope_ref[:, lanes] = normal + value * (jnp.exp(-0.5 * value * value) * 0.3989422804014327)
        total = total + dot(gate, down[lanes, :])
    sum_ref[...] = total


def feed_forward(at, mine, theirs, bias, up, down, rest, layer, after=()):
    right = block((TILE, D), lambda s: (0, 1))
    tokens = 2 * TILE
    return run(
        mlp_kernel,
        at,
        [(mine, right), (theirs, right), bias, *up_inputs(up, rest, layer), *down_inputs(down, rest, layer)],
        [shape((tokens, CORE_FF), BF16), shape((tokens, CORE_FF), F32), shape((tokens, D), F32)],
        "mlp",
        4 * tokens * D * CORE_FF,
        8500000,
        [pltpu.VMEM((tokens, D), BF16), pltpu.VMEM((D, CORE_FF), BF16), pltpu.VMEM((CORE_FF, D), BF16)],
        limit=40,
        exps=2 * tokens * CORE_FF,
        after=after,
    )


def key_range(pair):
    first = max(-1, 2 * pair - WINDOW // TILE)
    return first, 2 * pair + 2


PAIRS_OF_TILES = sum(2 * (key_range(pair)[1] - key_range(pair)[0]) for pair in range(TILES // 2))


def allowed_mask(pair, first, last, low_row, pos_row, place):
    parts = []
    for tile in range(first, last):
        ok = place >= low_row - TILE * tile
        if tile >= 2 * pair:
            ok = ok & (place <= pos_row - TILE * tile)
        parts.append(ok)
    return jnp.concatenate(parts, axis=0)


def unturned(grads, cosine, sine):
    low, high = grads[:8], grads[8:ROT]
    return jnp.concatenate(
        [low * cosine + high * sine, high * cosine - low * sine, grads[ROT:]], axis=0
    ).astype(BF16)


def attention_kernel(at, *refs, forward, backward):
    refs = list(refs)
    take = lambda count: [refs.pop(0) for _ in range(count)]
    got_ref, halo_ref, low_ref, pos_ref = take(4)
    if backward:
        cos_ref, sin_ref = take(2)
        if not forward:
            dctx_ref, saved_ctx, saved_lse = take(3)
    if forward and not backward:
        out_ref, ctx_ref, lse_ref = take(3)
    if backward:
        packed_ref, edge_ref, tail_ref = take(3)
    key_tok, query_t = take(2)
    if forward:
        (val_t,) = take(1)
    if backward:
        val_tok, key_t, query_tok, dctx_t, dctx_tok, dkv = take(6)

    reverse = at[REVERSE]
    place = lax.broadcasted_iota(jnp.int32, (TILE, 2 * TILE), 0) ^ at[SWAPPED]

    def chip(tile):
        return jnp.where(reverse == 1, TILES - 1 - tile, tile)

    for tile in range(-1, TILES):
        here = slice(tile * TILE, (tile + 1) * TILE)
        after = slice((tile + 1) * TILE, (tile + 2) * TILE)
        if tile < 0:
            key, val = halo_ref[0:HEAD, :], halo_ref[HEAD:, :]
        else:
            source = chip(tile)
            query, key, val = (got_ref[source, part * HEAD : (part + 1) * HEAD, :] for part in range(3))
            query_t[:, here] = query
            if backward:
                query_tok[here, :] = query.T
                dctx = got_ref[source, QKV:, :] if forward else dctx_ref[source]
                dctx_t[:, here] = dctx
                dctx_tok[here, :] = dctx.T
        key_tok[after, :] = key.T
        if forward:
            val_t[:, after] = val
        if backward:
            key_t[:, after] = key
            val_tok[after, :] = val.T
    if backward:
        dkv[...] = jnp.zeros_like(dkv)
    for pair in range(TILES // 2):
        first, last = key_range(pair)
        rows = slice((first + 1) * TILE, (last + 1) * TILE)
        lanes = slice(pair * 2 * TILE, (pair + 1) * 2 * TILE)
        places = chip(2 * pair), chip(2 * pair + 1)
        scores = dot(key_tok[rows, :], query_t[:, lanes])
        ok = allowed_mask(pair, first, last, low_ref[:, lanes], pos_ref[:, lanes], place)
        scores = jnp.where(ok, scores, BLOCKED)
        if forward:
            peak = jnp.max(scores, axis=0, keepdims=True)
            probs = jnp.exp(scores - peak)
            total = jnp.sum(probs, axis=0, keepdims=True)
            inverse = 1.0 / total
            ctx = dot(val_t[:, rows], probs.astype(BF16)) * inverse
            low_ctx = ctx.astype(BF16)
            for index in range(2):
                lanes_here = slice(index * TILE, (index + 1) * TILE)
                if backward:
                    packed_ref[places[index], QKV:, :] = low_ctx[:, lanes_here]
                else:
                    out_ref[places[index]] = low_ctx[:, lanes_here]
            if backward:
                probs = probs * inverse
            else:
                ctx_ref[:, lanes] = ctx
                lse_ref[:, lanes] = peak + jnp.log(total)
        else:
            probs = jnp.exp(scores - saved_lse[:, lanes])
            ctx = saved_ctx[:, lanes]
        if backward:
            dctx = dctx_t[:, lanes]
            dprobs = dot(val_tok[rows, :], dctx)
            delta = jnp.sum(ctx * dctx.astype(F32), axis=0, keepdims=True)
            dscores = (probs * (dprobs - delta)).astype(BF16)
            dquery = dot(key_t[:, rows], dscores) * 0.125
            dquery = unturned(dquery, cos_ref[:, lanes], sin_ref[:, lanes])
            packed_ref[places[0], 0:HEAD, :] = dquery[:, :TILE]
            packed_ref[places[1], 0:HEAD, :] = dquery[:, TILE:]
            dkv[rows, 0:HEAD] += dot(dscores, query_tok[lanes, :])
            dkv[rows, HEAD:] += dot(probs.astype(BF16), dctx_tok[lanes, :])
    if backward:
        edge_ref[...] = dkv[0:TILE, :]
        tail_ref[...] = dkv[TILES * TILE :, :]
        for tile in range(TILES - 1):
            lanes = slice(tile * TILE, (tile + 1) * TILE)
            grads = dkv[(tile + 1) * TILE : (tile + 2) * TILE, :].T
            packed_ref[chip(tile), HEAD:QKV, :] = unturned(grads, cos_ref[:, lanes], sin_ref[:, lanes])
        packed_ref[chip(TILES - 1), HEAD:QKV, :] = jnp.zeros((2 * HEAD, TILE), BF16)


def attention(at, got, halo, low, pos, tables=None, dctx=None, saved=None):
    forward, backward = saved is None, tables is not None
    keys = UNIT + TILE
    inputs = [got, halo, low, pos]
    outs = []
    scratch = [pltpu.VMEM((keys, HEAD), BF16), pltpu.VMEM((HEAD, UNIT), BF16)]
    if forward:
        scratch.append(pltpu.VMEM((HEAD, keys), BF16))
        if not backward:
            outs += [shape((TILES, HEAD, TILE), BF16), shape((HEAD, UNIT), F32), shape((1, UNIT), F32)]
    if backward:
        inputs += list(tables)
        if saved is not None:
            inputs += [dctx, *saved]
        rows = QKV + HEAD if forward else QKV
        outs += [shape((TILES, rows, TILE), BF16), shape((TILE, 2 * HEAD), F32), shape((TILE, 2 * HEAD), F32)]
        scratch += [
            pltpu.VMEM((keys, HEAD), BF16),
            pltpu.VMEM((HEAD, keys), BF16),
            pltpu.VMEM((UNIT, HEAD), BF16),
            pltpu.VMEM((HEAD, UNIT), BF16),
            pltpu.VMEM((UNIT, HEAD), BF16),
            pltpu.VMEM((keys, 2 * HEAD), F32),
        ]
    products = (2 if forward else 1) + (4 if backward else 0)
    return run(
        functools.partial(attention_kernel, forward=forward, backward=backward),
        at,
        inputs,
        outs,
        "attention" + ("_forward" if forward else "") + ("_backward" if backward else ""),
        2 * products * PAIRS_OF_TILES * TILE * TILE * HEAD * 4,
        4000000,
        scratch,
        exps=PAIRS_OF_TILES * TILE * TILE,
    )


def edge_kernel(at, packed_ref, tail_ref, edge_ref, cos_ref, sin_ref, out_ref):
    grads = tail_ref[...] + jnp.where(at[FIRST_HALF] == 1, edge_ref[...], 0.0)
    out_ref[0, 0:HEAD, :] = packed_ref[0, 0:HEAD, :]
    out_ref[0, HEAD:QKV, :] = unturned(grads.T, cos_ref[...], sin_ref[...])
    if out_ref.shape[1] > QKV:
        out_ref[0, QKV:, :] = packed_ref[0, QKV:, :]


def add_edge(at, packed, tail, edge, cosine, sine):
    spec = block((1,) + packed.shape[1:], lambda s: (s[LAST_CHIP], 0, 0))
    last = block((8, TILE), lambda s: (0, TILES - 1))
    return run(
        edge_kernel,
        at,
        [(packed, spec), tail, edge, (cosine, last), (sine, last)],
        [shape(packed.shape, BF16)],
        "attention_edge",
        100000,
        300000,
        limit=8,
        aliases={1: 0},
        out_specs=[spec],
    )[0]


def out_kernel(at, got_ref, own_ref, other_ref, sum_ref, keep_ref, give_ref, weights):
    fill_out(at[ZH], weights, own_ref, other_ref)
    rows = TILE // 2
    for seq in range(2):
        ctx = got_ref[seq * SLOTS : seq * SLOTS + CORE_HEADS].reshape(HALF, TILE)
        value = dot(ctx, weights[...], TN)
        here = slice(seq * rows, (seq + 1) * rows)
        there = slice(TILE + seq * rows, TILE + (seq + 1) * rows)
        keep_ref[here, :] = value[:rows] + sum_ref[here, :]
        give_ref[here, :] = value[rows:] + sum_ref[there, :]


def ctx_of(got):
    return got, block((TILES, HEAD, TILE), lambda s: (0, got.shape[1] // HEAD - 1, 0))


def attention_out(at, got, outs, total, layer, after=()):
    return run(
        out_kernel,
        at,
        [ctx_of(got), *out_inputs(*outs, layer), total],
        [shape((TILE, D), F32), shape((TILE, D), F32)],
        "attention_out",
        4 * TILE * HALF * D,
        2700000,
        [pltpu.VMEM((HALF, D), BF16)],
        after=after,
    )


def dctx_kernel(at, mine_ref, theirs_ref, own_ref, other_ref, out_ref, weights, tok):
    fill_out(at[ZH], weights, own_ref, other_ref)
    assemble(tok, mine_ref[...], theirs_ref[...])
    value = dot(weights[...], tok[...], NT).astype(BF16)
    for seq in range(2):
        part = value[:, seq * TILE : (seq + 1) * TILE].reshape(CORE_HEADS, HEAD, TILE)
        start = seq * SLOTS
        out_ref[start : start + CORE_HEADS] = part
        out_ref[start + CORE_HEADS : start + SLOTS] = jnp.zeros((SLOTS - CORE_HEADS, HEAD, TILE), BF16)


def grad_ctx(at, mine, theirs, outs, layer):
    return run(
        dctx_kernel,
        at,
        [mine, theirs, *out_inputs(*outs, layer)],
        [shape((TILES, HEAD, TILE), BF16)],
        "grad_ctx",
        4 * TILE * HALF * D,
        1300000,
        [pltpu.VMEM((HALF, D), BF16), pltpu.VMEM((2 * TILE, D), BF16)],
    )[0]


def put_early(z, act_mine, act_theirs, gate_ref, sent_ref):
    sent_ref[0:TILE, 0:HALF] = act_mine[:, half_at(1 - z)]
    sent_ref[TILE:, 0:HALF] = act_theirs[:, half_at(1 - z)]
    lanes = pl.ds(pl.multiple_of((1 - z) * QUARTER, QUARTER), QUARTER)
    sent_ref[:, SENT_GATE:SENT_CTX] = gate_ref[:, lanes]


def mlp_back_kernel(at, *refs, early):
    refs = list(refs)
    take = lambda count: [refs.pop(0) for _ in range(count)]
    mine_ref, theirs_ref, slope_ref, up0_ref, up1_ref, up_rest, down_own, down_rest = take(8)
    if early:
        act_mine, act_theirs, gate_ref = take(3)
    dup_ref, keep_ref, give_ref, bias_ref, sent_ref, dhid, up, down = refs
    z = at[ZH]
    dhid[0:TILE] = mine_ref[...]
    dhid[TILE:] = theirs_ref[...]
    fill_up(z, up, up0_ref, up1_ref, up_rest)
    fill_down(z, down, down_own, down_rest)
    total = jnp.zeros((2 * TILE, D), F32)
    start = SENT_CTX if early else 0
    for part in range(4):
        lanes = slice(part * HALF, (part + 1) * HALF)
        value = dot(dhid[...], down[lanes, :], NT) * slope_ref[:, lanes]
        dup = value.astype(BF16)
        dup_ref[:, lanes] = dup
        sent_ref[:, start + part * HALF : start + (part + 1) * HALF] = dup
        bias_ref[part : part + 1, :] = jnp.sum(dup.astype(F32), axis=0, keepdims=True)
        total = total + dot(dup, up[:, lanes], NT)
    keep_ref[...] = total[:TILE]
    give_ref[...] = total[TILE:]
    sent_ref[:, start + CORE_FF :] = dhid[...]
    if early:
        put_early(z, act_mine, act_theirs, gate_ref, sent_ref)


def mlp_back(at, mine, theirs, slope, up, down, rest, layer, early=None):
    right = block((TILE, D), lambda s: (0, 1))
    tokens = 2 * TILE
    extra = [] if early is None else [(early[0], right), (early[1], right), early[2]]
    width = SENT_LATE + (0 if early is None else SENT_CTX)
    return run(
        functools.partial(mlp_back_kernel, early=early is not None),
        at,
        [mine, theirs, slope, *up_inputs(up, rest, layer), *down_inputs(down, rest, layer), *extra],
        [
            shape((tokens, CORE_FF), BF16),
            shape((TILE, D), F32),
            shape((TILE, D), F32),
            shape((4, HALF), F32),
            shape((tokens, width), BF16),
        ],
        "mlp_back",
        4 * tokens * D * CORE_FF,
        8500000,
        [pltpu.VMEM((tokens, D), BF16), pltpu.VMEM((D, CORE_FF), BF16), pltpu.VMEM((CORE_FF, D), BF16)],
    )


def early_kernel(at, act_mine, act_theirs, gate_ref, ctx_ref, sent_ref):
    z = at[ZH]
    put_early(z, act_mine, act_theirs, gate_ref, sent_ref)
    for seq in range(2):
        ctx = ctx_ref[pl.ds(seq * SLOTS + 3 * (1 - z), 3)].reshape(QKV, TILE)
        sent_ref[seq * TILE : (seq + 1) * TILE, SENT_CTX : SENT_CTX + QKV] = ctx.T
    sent_ref[:, SENT_CTX + QKV :] = jnp.zeros((2 * TILE, HEAD), BF16)


def pack_early(at, mine, theirs, gate, ctx):
    right = block((TILE, D), lambda s: (0, 1))
    outs = [shape((2 * TILE, SENT_EARLY), BF16)]
    return run(early_kernel, at, [(mine, right), (theirs, right), gate, ctx], outs, "pack_early", 0, 0)[0]


def put_out_grads(grads, ctx_ref, tok, z, offset, length):
    for side in range(2):
        lanes = slice(side * HALF, (side + 1) * HALF)
        value = jnp.zeros((QKV, HALF), F32)
        for seq in range(2):
            ctx = ctx_ref[seq * SLOTS + 3 * z : seq * SLOTS + 3 * z + 3].reshape(QKV, TILE)
            value = value + dot(ctx, tok[seq * TILE : (seq + 1) * TILE, lanes])
        value = value.astype(BF16)
        for index in range(2):
            start = (2 * side + index) * length + offset
            grads[start : start + OUT_PART, :] = value[index * OUT_PART : (index + 1) * OUT_PART]


def by_chunks(grads, out_ref, length):
    out_ref[...] = grads[...].reshape(16, length // 4, HALF)


def own_grads_kernel(at, act_mine, act_theirs, mine_ref, theirs_ref, gate_ref, dup_ref, *refs, with_ctx):
    refs = list(refs)
    if with_ctx:
        ctx_ref, early_ref, late_ref, out_ref, done_ref, act, dhid, grads, tok, tok_other = refs
        length, start = PART_FIRST, 0
    else:
        late_ref, out_ref, done_ref, act, dhid, grads = refs
        early_ref = late_ref
        length, start = PART_SECOND, SENT_CTX
    z = at[ZH]
    done_ref[...] = jnp.zeros_like(done_ref)
    act[0:TILE] = act_mine[:, half_at(z)]
    act[TILE:] = act_theirs[:, half_at(z)]
    dhid[0:TILE] = mine_ref[...]
    dhid[TILE:] = theirs_ref[...]
    act_t, act_other = act[...].T, early_ref[:, 0:HALF].T
    for part in range(4):
        lanes = slice(part * HALF, (part + 1) * HALF)
        other = slice(start + part * HALF, start + (part + 1) * HALF)
        value = dot(act_t, dup_ref[:, lanes]) + dot(act_other, late_ref[:, other])
        grads[part * length : part * length + HALF, :] = value.astype(BF16)
    start += CORE_FF
    gate_t = gate_ref[:, pl.ds(pl.multiple_of(z * QUARTER, QUARTER), QUARTER)].T
    gate_other = early_ref[:, SENT_GATE:SENT_CTX].T
    for side in range(2):
        lanes = slice(side * HALF, (side + 1) * HALF)
        other = slice(start + side * HALF, start + (side + 1) * HALF)
        value = (dot(gate_t, dhid[:, lanes]) + dot(gate_other, late_ref[:, other])).astype(BF16)
        for index in range(2):
            row = (2 * side + index) * length + HALF
            grads[row : row + HALF, :] = value[index * HALF : (index + 1) * HALF]
    if with_ctx:
        assemble(tok, mine_ref[...], theirs_ref[...])
        assemble(tok_other, late_ref[0:TILE, start:], late_ref[TILE:, start:])
        ctx_other = early_ref[:, SENT_CTX : SENT_CTX + QKV].T
        for side in range(2):
            lanes = slice(side * HALF, (side + 1) * HALF)
            value = dot(ctx_other, tok_other[:, lanes])
            for seq in range(2):
                ctx = ctx_ref[pl.ds(seq * SLOTS + 3 * z, 3)].reshape(QKV, TILE)
                value = value + dot(ctx, tok[seq * TILE : (seq + 1) * TILE, lanes])
            value = value.astype(BF16)
            for index in range(2):
                row = (2 * side + index) * length + 2 * HALF
                grads[row : row + OUT_PART, :] = value[index * OUT_PART : (index + 1) * OUT_PART]
                grads[row + OUT_PART : row + OUT_PART + 32, :] = jnp.zeros((32, HALF), BF16)
    by_chunks(grads, out_ref, length)


def own_grads(at, mine, theirs, dmine, dtheirs, gate, dup, late, early=None, ctx=None):
    right = block((TILE, D), lambda s: (0, 1))
    tokens = 2 * TILE
    length = PART_SECOND if ctx is None else PART_FIRST
    inputs = [(mine, right), (theirs, right), dmine, dtheirs, gate, dup]
    inputs += [late] if ctx is None else [ctx, early, late]
    scratch = [pltpu.VMEM((tokens, HALF), BF16), pltpu.VMEM((tokens, D), BF16), pltpu.VMEM((4 * length, HALF), BF16)]
    if ctx is not None:
        scratch += [pltpu.VMEM((tokens, D), BF16)] * 2
    return run(
        functools.partial(own_grads_kernel, with_ctx=ctx is not None),
        at,
        inputs,
        [shape((16, length // 4, HALF), BF16), shape((8, 128), F32)],
        "own_grads",
        4 * tokens * 4 * length * HALF,
        8000000,
        scratch,
        token=True,
    )[0]


def grads_qkv_kernel(
    at, got_ref, mine_ref, theirs_ref, dmine_ref, dtheirs_ref, ctx_ref, out_ref, done_ref, act, tok, grads
):
    done_ref[...] = jnp.zeros_like(done_ref)
    assemble(act, mine_ref[...], theirs_ref[...])
    assemble(tok, dmine_ref[...], dtheirs_ref[...])
    for z in range(2):
        put_out_grads(grads, ctx_ref, tok, z, QKV_PART, PART_QKV)
        lanes = slice(z * HALF, (z + 1) * HALF)
        value = jnp.zeros((QKV_ROWS, HALF), F32)
        for seq in range(2):
            rows = got_ref[seq * SLOTS : seq * SLOTS + CORE_HEADS, 0:QKV, :].reshape(QKV_ROWS, TILE)
            value = value + dot(rows, act[seq * TILE : (seq + 1) * TILE, lanes])
        value = value.astype(BF16)
        for part in range(4):
            start = part * PART_QKV
            grads[start : start + QKV_PART, :] = value[part * QKV_PART : (part + 1) * QKV_PART]
        out_ref[:, z] = grads[...].reshape(16, CHUNK_QKV, HALF)


def grads_qkv(at, got, mine, theirs, dmine, dtheirs):
    left = block((TILE, D), lambda s: (0, 0))
    return run(
        grads_qkv_kernel,
        at,
        [got, (mine, left), (theirs, left), dmine, dtheirs, ctx_of(got)],
        [shape((16, 2, CHUNK_QKV, HALF), BF16), shape((8, 128), F32)],
        "grads_qkv",
        4 * TILE * D * 4 * PART_QKV,
        3800000,
        [pltpu.VMEM((2 * TILE, D), BF16)] * 2 + [pltpu.VMEM((4 * PART_QKV, HALF), BF16)],
        token=True,
    )[0]


def spread_kernel(at, *refs):
    outs = refs[8:]
    rows = outs[0].shape[0] // 4
    for index, axis in ((0, RING_Y), (1, RING_X)):
        for step in range(4):
            place = (at[axis] + 4 - step) % 4
            outs[index][pl.ds(pl.multiple_of(place * rows, 32), rows), :] = refs[4 * index + step][...]


def spread(at, pieces, after):
    rows = pieces[0].shape[0]
    outs = [shape((4 * rows, HALF), BF16)] * 2
    return run(spread_kernel, at, pieces, outs, "ring_spread", 0, 32 * rows * HALF, after=after)


def collect_kernel(at, *refs):
    out_ref = refs[8]
    rows = refs[0].shape[0] // 4
    for step in range(4):
        x = (at[RING_X] + 4 - step) % 4
        for y in range(4):
            to = pl.ds(pl.multiple_of((x * 4 + y) * 2 * rows, 32), rows)
            out_ref[to, :] = refs[step][y * rows : (y + 1) * rows, :]
        y = (at[RING_Y] + 4 - step) % 4
        for x in range(4):
            to = pl.ds(pl.multiple_of((x * 4 + y) * 2 * rows + rows, 32), rows)
            out_ref[to, :] = refs[4 + step][x * rows : (x + 1) * rows, :]


def collect(at, pieces, after):
    rows = pieces[0].shape[0]
    outs = [shape((8 * rows, HALF), BF16)]
    return run(collect_kernel, at, pieces, outs, "ring_collect", 0, 32 * rows * HALF, after=after)[0]


def qkv_back_kernel(at, got_ref, own_ref, other_ref, keep_ref, give_ref, bias_ref):
    z = at[ZH]
    rows = TILE // 2
    sums = jnp.zeros((8, QKV_ROWS), F32)
    for seq in range(2):
        tok = got_ref[seq * SLOTS : seq * SLOTS + CORE_HEADS, 0:QKV, :].reshape(QKV_ROWS, TILE).T
        sums = sums + dot(jnp.ones((8, TILE), BF16), tok)
        here = slice(seq * rows, (seq + 1) * rows)
        for weights, at_z in ((own_ref, z), (other_ref, 1 - z)):
            value = dot(tok, weights[...])
            keep_ref[here, half_at(at_z)] = value[:rows]
            give_ref[here, half_at(at_z)] = value[rows:]
    bias_ref[...] = sums


def qkv_back(at, got, own, other):
    return run(
        qkv_back_kernel,
        at,
        [got, turned(own), turned(other)],
        [shape((TILE, D), F32), shape((TILE, D), F32), shape((8, QKV_ROWS), F32)],
        "qkv_back",
        4 * TILE * D * QKV_ROWS,
        3500000,
        limit=24,
    )


def qkv_rows(got_ref, tok, out_ref):
    for z in range(2):
        lanes = slice(z * HALF, (z + 1) * HALF)
        value = jnp.zeros((QKV_ROWS, HALF), F32)
        for seq in range(2):
            grads = got_ref[seq * SLOTS : seq * SLOTS + CORE_HEADS].reshape(QKV_ROWS, TILE)
            value = value + dot(grads, tok[seq * TILE : (seq + 1) * TILE, lanes])
        out_ref[z, 0:QKV_ROWS, :] = value.astype(BF16)


def qkv_grads_first_kernel(at, got_ref, mine_ref, theirs_ref, *refs):
    sums, (out_ref, tok, small) = refs[:6], refs[6:]
    assemble(tok, mine_ref[...], theirs_ref[...])
    qkv_rows(got_ref, tok, out_ref)

    def by_core(core):
        for z in range(2):
            small[...] = jnp.zeros((4 * SMALL, HALF), F32)
            for layer in range(LAYERS):
                norm_ref, up_ref, qkv_ref = sums[3 * layer : 3 * layer + 3]
                start = layer * SMALL
                for index in range(5):
                    small[start + index : start + index + 1] = norm_ref[2 * index + z : 2 * index + z + 1]
                for index in range(3):
                    part, half = (3 * z + index) // 2, (3 * z + index) % 2
                    for head in range(3):
                        lane = core * QKV + head * HEAD
                        source = (3 * half + head) * QKV + part * HEAD
                        small[start + 5 + index : start + 6 + index, lane : lane + HEAD] = qkv_ref[
                            0:1, source : source + HEAD
                        ]
                for side in range(2):
                    row = start + 8 + 2 * core + side
                    small[row : row + 1] = up_ref[2 * z + side : 2 * z + side + 1]
            out_ref[z, QKV_ROWS : QKV_ROWS + 4 * SMALL, :] = small[...].astype(BF16)
            used = QKV_ROWS + 4 * SMALL
            out_ref[z, used:, :] = jnp.zeros((QKV_FIRST - used, HALF), BF16)

    for core in range(2):
        pl.when(at[CORE] == core)(functools.partial(by_core, core))


def qkv_grads_first(at, got, mine, theirs, sums, after):
    left = block((TILE, D), lambda s: (0, 0))
    return run(
        qkv_grads_first_kernel,
        at,
        [got, (mine, left), (theirs, left), *sums],
        [shape((2, QKV_FIRST, HALF), BF16)],
        "qkv_grads_first",
        4 * TILE * D * QKV_ROWS,
        3300000,
        [pltpu.VMEM((2 * TILE, D), BF16), pltpu.VMEM((4 * SMALL, HALF), F32)],
        after=after,
    )[0]


def norm_back_kernel(
    at, keep0, got0, keep1, got1, hat_ref, inverse_ref, gain_ref, dstream_ref, next_ref, low_ref, sums_ref
):
    first, second = keep0[...] + got0[...], keep1[...] + got1[...]
    hat = hat_ref[...]
    dstream = dstream_ref[...].astype(F32)
    dhat = first * gain_ref[0:1] + second * gain_ref[1:2]
    grad = inverse_ref[...] * (
        dhat
        - jnp.mean(dhat, axis=-1, keepdims=True)
        - hat * jnp.mean(dhat * hat, axis=-1, keepdims=True)
    )
    total = dstream + grad
    next_ref[...] = total
    low_ref[...] = total.astype(BF16)
    rows = (first * hat, second * hat, first, second, dstream.astype(BF16).astype(F32))
    for index, value in enumerate(rows):
        row = jnp.sum(value, axis=0, keepdims=True)
        sums_ref[2 * index : 2 * index + 1, :] = row[:, :HALF]
        sums_ref[2 * index + 1 : 2 * index + 2, :] = row[:, HALF:]


def norm_back(at, first, second, hat, inverse, gain, dstream):
    return run(
        norm_back_kernel,
        at,
        [*first, *second, hat, inverse, gain, dstream],
        [shape((TILE, D), F32), shape((TILE, D), BF16), shape((10, HALF), F32)],
        "norm_back",
        2000000,
        3400000,
        limit=24,
    )


def rows_of(part, start, count, chunk, length, offset=0):
    at = start
    while at < start + count:
        step = min(chunk - at % chunk, start + count - at)
        yield (4 * part + at // chunk) * length + offset + at % chunk, at - start, step
        at += step


def place_mlp(source, core, up_ref, down_ref, chunk, length):
    for part in range(4):
        z, side = part // 2, part % 2
        column = z * CORE_FF + core * QUARTER + side * HALF
        for source_row, row, count in rows_of(part, 0, HALF, chunk, length):
            up_ref[0, row : row + count, column : column + HALF] = source[source_row : source_row + count, :].astype(F32)
        side, index = part // 2, part % 2
        lanes = slice(side * HALF, (side + 1) * HALF)
        first = core * QUARTER + index * HALF
        for source_row, row, count in rows_of(part, HALF, HALF, chunk, length):
            row += first
            down_ref[0, row : row + count, lanes] = source[source_row : source_row + count, :].astype(F32)


def for_cores(at, mine, theirs, put):
    for here, source in ((True, mine), (False, theirs)):
        for core in range(2):
            pl.when((at[CORE] == core) == here)(functools.partial(put, core, source))


UP_SHAPE, DOWN_SHAPE, OUT_SHAPE = (LAYERS, HALF, FF), (LAYERS, FF // 2, D), (LAYERS, HALF, D)
QKV_SHAPE = (LAYERS, HALF, 3 * D)
PLACED = (UP_SHAPE, DOWN_SHAPE, OUT_SHAPE)


def place_out(source, core, out_ref, first, chunk, length, offset):
    for part in range(4):
        lanes = slice((part // 2) * HALF, (part // 2 + 1) * HALF)
        start = core * QKV + (part % 2) * OUT_PART
        for source_row, row, count in rows_of(part, first, OUT_PART, chunk, length, offset):
            row += start
            out_ref[0, row : row + count, lanes] = source[source_row : source_row + count, :].astype(F32)


def place_turned(rows_ref, out_ref, part, z):
    column = part * D + z * HALF
    out_ref[0, :, column : column + HALF] = rows_ref[...].T


def place_second_kernel(at, mine_ref, theirs_ref, up_ref, down_ref, done_ref):
    done_ref[...] = jnp.zeros_like(done_ref)
    for_cores(
        at,
        mine_ref,
        theirs_ref,
        lambda core, source: place_mlp(source, core, up_ref, down_ref, CHUNK_SECOND, CHUNK_SECOND),
    )


def place_second(at, mine, theirs):
    outs = PLACED[:2]
    return run(
        place_second_kernel,
        at,
        [mine, theirs],
        [shape(dims, F32) for dims in outs] + [shape((8, 128), F32)],
        "place_second",
        0,
        14000000,
        out_specs=[block((1,) + dims[1:], lambda s: (1, 0, 0)) for dims in outs] + [block((8, 128))],
        token=True,
    )[:-1]


def place_first_kernel(
    at, mine_ref, theirs_ref, up_in, down_in, qkv_in, up_ref, down_ref, out_ref, qkv_ref, done_ref, rows_ref
):
    length = CHUNK_FIRST + CHUNK_QKV
    done_ref[...] = jnp.zeros_like(done_ref)

    def put(core, source):
        place_mlp(source, core, up_ref, down_ref, CHUNK_FIRST, length)
        place_out(source, core, out_ref.at[0:1], 2 * HALF, CHUNK_FIRST, length, 0)
        place_out(source, core, out_ref.at[1:2], QKV_PART, CHUNK_QKV, length, CHUNK_FIRST)

    for_cores(at, mine_ref, theirs_ref, put)
    for part in range(3):
        for z in range(2):

            def put_rows(core, source):
                for head in range(3):
                    row = (z * 3 + head) * QKV + part * HEAD
                    to = core * QKV + head * HEAD
                    for first in range(row, row + HEAD, 32):
                        pieces = rows_of(first // QKV_PART, first % QKV_PART, 32, CHUNK_QKV, length, CHUNK_FIRST)
                        for source_row, more, count in pieces:
                            here = to + first - row + more
                            rows_ref[here : here + count, :] = source[source_row : source_row + count, :].astype(F32)

            for_cores(at, mine_ref, theirs_ref, put_rows)
            place_turned(rows_ref, qkv_ref, part, z)


def place_first(at, mine, theirs, up, down, qkv):
    anywhere = pl.BlockSpec(memory_space=pl.ANY)
    return run(
        place_first_kernel,
        at,
        [mine, theirs, (up, anywhere), (down, anywhere), (qkv, anywhere)],
        [shape(dims, F32) for dims in (*PLACED, QKV_SHAPE)] + [shape((8, 128), F32)],
        "place_first",
        0,
        24000000,
        [pltpu.VMEM((HALF, HALF), F32)],
        aliases={3: 0, 4: 1, 5: 3},
        out_specs=[
            block((1,) + UP_SHAPE[1:], lambda s: (0, 0, 0)),
            block((1,) + DOWN_SHAPE[1:], lambda s: (0, 0, 0)),
            block(OUT_SHAPE),
            block((1,) + QKV_SHAPE[1:], lambda s: (1, 0, 0)),
            block((8, 128)),
        ],
        token=True,
    )[:-1]


def place_qkv_kernel(
    at, mine_ref, theirs_ref, out_ref, gain_ref, offset_ref, hidden_ref, again_ref, qkv_ref, up_ref, rows_ref
):
    for part in range(3):
        for z in range(2):

            def put(core, source):
                for head in range(3):
                    row = (z * 3 + head) * QKV + part * HEAD
                    to = core * QKV + head * HEAD
                    rows_ref[to : to + HEAD, :] = source[row : row + HEAD, :].astype(F32)

            for_cores(at, mine_ref, theirs_ref, put)
            place_turned(rows_ref, out_ref, part, z)
    rows = slice(QKV_ROWS, QKV_ROWS + 2 * SMALL + 8)
    small = mine_ref[rows, :].astype(F32) + theirs_ref[rows, :].astype(F32)
    for layer in range(LAYERS):
        start = layer * SMALL
        gain_ref[layer] = small[start : start + 2]
        offset_ref[layer] = small[start + 2 : start + 4]
        hidden_ref[layer : layer + 1] = small[start + 4 : start + 5]
        again_ref[layer : layer + 1] = small[start + 4 : start + 5]
        for index in range(3):
            lanes = slice(index * HALF, (index + 1) * HALF)
            qkv_ref[layer : layer + 1, lanes] = small[start + 5 + index : start + 6 + index]
        for index in range(4):
            lanes = slice(index * HALF, (index + 1) * HALF)
            up_ref[layer : layer + 1, lanes] = small[start + 8 + index : start + 9 + index]


def place_qkv(at, mine, theirs):
    outs = [shape((LAYERS, HALF, 3 * D), F32)]
    specs = [block((1, HALF, 3 * D), lambda s: (0, 0, 0))]
    for dims in ((2, HALF), (2, HALF), (HALF,), (HALF,), (3 * HALF,), (4 * HALF,)):
        outs.append(shape((LAYERS,) + dims, F32))
        specs.append(block((LAYERS,) + dims))
    return run(
        place_qkv_kernel,
        at,
        [mine, theirs],
        outs,
        "place_qkv",
        0,
        6000000,
        [pltpu.VMEM((HALF, HALF), F32)],
        limit=40,
        out_specs=specs,
    )


ROW_GAIN, ROW_OFFSET, ROW_QKV, ROW_OUT, ROW_UP, ROW_DOWN, SMALL_ROWS = 0, 4, 8, 14, 16, 24, 32


def gather_small(refs):
    gain, offset, qkv, out, up, down = (ref[...].astype(F32) for ref in refs)
    rows = [gain.reshape(4, HALF), offset.reshape(4, HALF)]
    rows += [qkv[layer : layer + 1, part * HALF : (part + 1) * HALF] for layer in range(LAYERS) for part in range(3)]
    rows.append(out)
    rows += [up[layer : layer + 1, part * HALF : (part + 1) * HALF] for layer in range(LAYERS) for part in range(4)]
    rows += [down, jnp.zeros((SMALL_ROWS - ROW_DOWN - LAYERS, HALF), F32)]
    return jnp.concatenate(rows, axis=0)


def spread_small_kernel(at, own_ref, other_ref, *outs):
    own, other = own_ref[...].astype(F32), other_ref[...].astype(F32)
    swap = at[ZH] == 1
    halves = jnp.where(swap, other, own), jnp.where(swap, own, other)

    def row(index, z):
        return halves[z][index : index + 1]

    def by_core(core):
        for layer in range(LAYERS):
            qkv_ref, up_ref = outs[5 * layer + 2], outs[5 * layer + 4]
            for part in range(3):
                for z in range(2):
                    place = part * 2 + z
                    values = row(ROW_QKV + layer * 3 + place % 3, place // 3)
                    for head in range(3):
                        lane = core * QKV + head * HEAD
                        qkv_ref[3 * z + head : 3 * z + head + 1, part * HEAD : (part + 1) * HEAD] = values[
                            :, lane : lane + HEAD
                        ]
            for z in range(2):
                for side in range(2):
                    lane = z * QUARTER + side * HALF
                    up_ref[:, lane : lane + HALF] = row(ROW_UP + 4 * layer + 2 * core + side, z)

    for core in range(2):
        pl.when(at[CORE] == core)(functools.partial(by_core, core))
    for layer in range(LAYERS):
        gain_ref, offset_ref, _, rest_ref, _ = outs[5 * layer : 5 * layer + 5]
        for z in range(2):
            lanes = slice(z * HALF, (z + 1) * HALF)
            for index in range(2):
                gain_ref[index : index + 1, lanes] = row(ROW_GAIN + 2 * layer + index, z)
                offset_ref[index : index + 1, lanes] = row(ROW_OFFSET + 2 * layer + index, z)
            rest_ref[:, lanes] = row(ROW_OUT + layer, z) + row(ROW_DOWN + layer, z)


def spread_small(at, rows, other):
    outs = [shape((2, D), F32), shape((2, D), F32), shape((8, QKV), F32), shape((1, D), F32), shape((1, CORE_FF), F32)]
    spec = block((SMALL_ROWS, HALF), lambda s: (QKV_ROWS // SMALL_ROWS, 0))
    values = run(spread_small_kernel, at, [(rows, spec), (other, spec)], outs * LAYERS, "small_spread", 0, 0)
    return zip(values[:5], values[5:])


EVERY = ("zh", "xh", "xl", "y", "zl")
ACROSS = ("xh", "xl", "y")
CHIPS = ("xl", "zl", "y")


def exchange(values):
    return lax.ppermute(values, "core", SWAP)


def scatter_sum(grads):
    parts = grads.reshape(64, -1, HALF)
    parts = lax.all_to_all(parts, EVERY, 0, 0, tiled=True)
    return jnp.sum(parts.astype(F32), axis=0).astype(BF16)


def add_from(part, other):
    return (part.astype(F32) + other.astype(F32)).astype(BF16)


def ring(values, axis, by):
    return lax.ppermute(values, axis, [(place, (place + by) % 4) for place in range(4)])


X_RING, Y_RING = ("xh", "xl"), "y"


def around(pieces, first, second):
    return [
        (ring(piece, first if index < 4 else second, index % 4) if index % 4 else piece)
        for index, piece in enumerate(pieces)
    ]


def sum_x(grads):
    return lax.psum_scatter(grads.reshape(-1, HALF), X_RING, scatter_dimension=0, tiled=True)


def sum_y(part):
    return lax.psum_scatter(part, Y_RING, scatter_dimension=0, tiled=True)


def sum_grid(grads):
    parts = lax.all_to_all(grads, ACROSS, 0, 0, tiled=True)
    return jnp.sum(parts.astype(F32), axis=0).astype(BF16)


def sum_near(part):
    return add_from(part, lax.ppermute(part, "zl", SWAP))


def sum_depth(zh, part):
    part = part.reshape(2, -1, HALF)
    keep = jnp.where(zh == 0, part[0], part[1])
    give = jnp.where(zh == 0, part[1], part[0])
    near = lax.ppermute(keep, "zl", SWAP)
    far = lax.ppermute(give, "zh", SWAP)
    across = lax.ppermute(give, ("zl", "zh"), [(0, 3), (3, 0), (1, 2), (2, 1)])
    total = (keep.astype(F32) + near.astype(F32)) + (far.astype(F32) + across.astype(F32))
    return total.astype(BF16)


def gather_half(at, total, after):
    rows = total.shape[0] // 2
    halves = total[:rows], total[rows:]
    return spread(at, around([halves[0]] * 4 + [halves[1]] * 4, Y_RING, X_RING), after)


def gather_rest(at, long, after):
    return collect(at, around([long[0]] * 4 + [long[1]] * 4, X_RING, Y_RING), after)


def gather_short(part):
    copies = jnp.broadcast_to(part[None], (32,) + part.shape)
    return lax.all_to_all(copies, EVERY[1:], 0, 0, tiled=True).reshape(-1, HALF)


def token_places(offsets, lengths):
    ends = jnp.cumsum(lengths)
    before = ends[:, None] <= offsets[None, :]
    start = jnp.max(jnp.where(before, ends[:, None], 0), axis=0)
    return start, offsets >= ends[DOCS - 2]


def rotary(places):
    frequency = 1.0 / 10000.0 ** (jnp.arange(0, ROT, 2).astype(F32) / ROT)
    angles = frequency[:, None] * places.astype(F32)[None, :]
    return jnp.cos(angles), jnp.sin(angles)


def local(
    hidden_in,
    doc_lengths,
    norm_gain,
    norm_bias,
    qkv_weight,
    qkv_bias,
    out_weight,
    out_bias,
    up_weight,
    up_bias,
    down_weight,
    down_bias,
    cotangent,
):
    LATEST.clear()
    zh, core, xh, xl, zl, y = (lax.axis_index(name) for name in ("zh", "core", "xh", "xl", "zl", "y"))
    chip = (xl * 2 + zl) * 4 + y
    x = xh * 2 + xl
    lengths = doc_lengths[0]

    unit_seq = xl
    unit_half = jnp.where(unit_seq == 0, xh, 1 - xh)
    unit_swap = jnp.where(unit_seq == core, 0, TILE // 2)
    last_chip = jnp.where(unit_seq == 0, TILES - 1, 0)
    at = jnp.stack(
        [core, zh, unit_seq, unit_swap, 1 - unit_half, last_chip, x, y, x * 4 + y]
    ).astype(jnp.int32)

    lane = jnp.arange(TILE, dtype=jnp.int32)
    seq0_tile = xh * TILES + chip
    places = []
    for seq, tile in ((0, seq0_tile), (1, 2 * TILES - 1 - seq0_tile)):
        offsets = tile * TILE + (lane ^ jnp.where(seq == core, 0, TILE // 2))
        places.append(offsets - token_places(offsets, lengths[seq])[0])
    own_tables = rotary(jnp.concatenate(places))
    unit_lengths = lax.dynamic_index_in_dim(lengths, unit_seq, 0, keepdims=False)
    relative = (jnp.arange(TILES, dtype=jnp.int32)[:, None] * TILE + (lane ^ unit_swap)[None, :]).reshape(-1)
    offsets = unit_half * UNIT + relative
    start, padding = token_places(offsets, unit_lengths)
    unit_tables = rotary(offsets - start)
    low = jnp.where(padding, offsets, jnp.maximum(start, offsets - (WINDOW - 1)))
    low = (low - unit_half * UNIT).reshape(1, UNIT)
    pos = relative.reshape(1, UNIT)

    def to_units(values):
        return lax.all_to_all(values.reshape(TILES, -1, TILE), CHIPS, 0, 0, tiled=True)

    def halo_of(got):
        last = lax.dynamic_index_in_dim(got, last_chip, 0, keepdims=False)
        return lax.ppermute(last[HEAD:QKV], "xh", SWAP)

    def finish_attention(packed, edge, tail):
        edge = lax.ppermute(edge, "xh", SWAP)
        return to_units(add_edge(at, packed, tail, edge, *unit_tables))

    small = (norm_gain, norm_bias, qkv_bias, out_bias, up_bias, down_bias)

    def gather_chunks(chunk):
        return lax.all_gather(chunk, ACROSS, axis=0, tiled=True).reshape(16, CHUNK, HALF)

    weights = begin(at, qkv_weight, up_weight, down_weight, small)
    own_qkv, other_qkv = [weights], [lax.ppermute(weights, "zh", SWAP)]
    rest = [gather_chunks(other_qkv[0][CHUNK_AT:])]
    tokens = cotangent[0]
    dhid1 = (tokens, exchange(tokens))
    gain, offset, b_qkv, b_rest, b_up = spread_small(at, weights, other_qkv[0])
    _, hat0, inverse0, act = norms(at, hidden_in[0], None, gain[0], offset[0])
    acts0 = (act, exchange(act))
    got0 = to_units(project_qkv(at, *acts0, own_qkv[0], other_qkv[0], b_qkv[0], *own_tables))
    rows, weights = begin_rest(at, qkv_weight, up_weight, down_weight, out_weight)
    rows, weights = held(at, [rows, weights], (got0,))
    rows = lax.ppermute(rows, "zh", SWAP)
    own_qkv.append(weights)
    other_qkv.append(lax.ppermute(weights, "zh", SWAP))
    outs = (out_weight, rows)
    halo0 = halo_of(got0)
    ctx0, *saved0 = attention(at, got0, halo0, low, pos)
    rest.append(gather_chunks(held(at, [rows[REST_CHUNK:]])[0]))
    ctx0 = to_units(ctx0)
    gate0, slope0, total = feed_forward(at, *acts0, b_up[0], up_weight, down_weight, rest, 0)
    dctx1 = grad_ctx(at, *dhid1, outs, 1)
    keep, give = attention_out(at, ctx0, outs, total, 0)
    added = (keep, exchange(give), b_rest[0])

    stream, hat1, inverse1, act = norms(at, hidden_in[0], added, gain[1], offset[1])
    acts1 = (act, exchange(act))
    got1 = to_units(project_qkv(at, *acts1, own_qkv[1], other_qkv[1], b_qkv[1], *own_tables, dctx1))
    gate1, slope1, total = feed_forward(at, *acts1, b_up[1], up_weight, down_weight, rest, 1)
    dup1, keep, give, sum_up1, sent = mlp_back(
        at, *dhid1, slope1, up_weight, down_weight, rest, 1, (*acts1, gate1)
    )
    second1 = (keep, exchange(give))
    late1 = lax.ppermute(held(at, [sent], (got1,))[0], "zh", SWAP)
    halo1 = halo_of(got1)
    packed = attention(at, got1, halo1, low, pos, unit_tables)
    dqkv1 = finish_attention(*packed)
    grads1 = own_grads(at, *acts1, *dhid1, gate1, dup1, late1)
    part1 = sum_x(held(at, [grads1], (dqkv1,))[0])
    keep, give, sum_qkv1 = qkv_back(at, dqkv1, own_qkv[1], other_qkv[1])
    first1 = (keep, exchange(give))
    early0 = lax.ppermute(pack_early(at, *acts0, gate0, ctx0), "zh", SWAP)
    dstream, low_stream, sum_norm1 = norm_back(at, first1, second1, hat1, inverse1, gain[1], tokens)

    dhid0 = (low_stream, exchange(low_stream))
    dctx0 = to_units(grad_ctx(at, *dhid0, outs, 0))
    dup0, keep, give, sum_up0, sent = mlp_back(at, *dhid0, slope0, up_weight, down_weight, rest, 0)
    second0 = (keep, exchange(give))
    gradsq = grads_qkv(at, dqkv1, *acts1, *dhid1)
    gradsq, sent, part1 = held(at, [gradsq, sent, part1], (dctx0, early0))
    late0 = lax.ppermute(sent, "zh", SWAP)
    part1 = sum_y(part1)
    partq = sum_x(gradsq)
    packed = attention(at, got0, halo0, low, pos, unit_tables, dctx0, saved0)
    dqkv0 = finish_attention(*packed)
    grads0 = own_grads(at, *acts0, *dhid0, gate0, dup0, late0, early0, ctx0)
    part0 = sum_grid(held(at, [grads0], (dqkv0,))[0])
    keep, give, sum_qkv0 = qkv_back(at, dqkv0, own_qkv[0], other_qkv[0])
    first0 = (keep, exchange(give))
    dstream, _, sum_norm0 = norm_back(at, first0, second0, hat0, inverse0, gain[0], dstream)
    hidden_grad = dstream[None]
    partq, part1 = held(at, [partq, part1])
    partq = sum_y(partq)

    sums = (sum_norm0, sum_up0, sum_qkv0, sum_norm1, sum_up1, sum_qkv1)
    part_qkv = scatter_sum(qkv_grads_first(at, dqkv0, *acts0, sums, (part0,)))
    keep, give = attention_out(at, dqkv1, outs, total, 1)
    partq, part1 = held(at, [partq, part1])
    long1 = lax.all_gather(sum_near(part1), ACROSS, axis=0, tiled=True)
    hidden_out = (stream + (keep + exchange(give) + b_rest[1])).astype(BF16)[None]
    total0 = jnp.concatenate([sum_near(part0), sum_depth(zh, partq)])
    half0 = gather_half(at, total0, (part_qkv,))
    long1 = held(at, [long1])[0]
    qkv0 = gather_short(part_qkv)
    g_up, g_down = place_second(at, long1, exchange(long1))
    long0 = gather_rest(at, half0, (qkv0,))
    g_qkv, g_gain, g_offset, g_hidden, g_again, g_bqkv, g_bup = place_qkv(at, qkv0, exchange(qkv0))
    g_up, g_down, g_out, g_qkv = place_first(at, long0, exchange(long0), g_up, g_down, g_qkv)
    return (
        hidden_out,
        hidden_grad,
        g_gain,
        g_offset,
        g_qkv,
        g_bqkv,
        g_out,
        g_hidden,
        g_up,
        g_bup,
        g_down,
        g_again,
    )


def solution(mesh):
    fine = Mesh(
        mesh.devices.reshape(2, 2, 2, 4, 2, 2), ("xh", "xl", "zl", "y", "core", "zh")
    )
    ctx = ("xh", "xl", "zl", "y", "core")
    rows = P(None, "zh", None)
    tokens = P("zh", ctx, None)
    last = P(None, None, "zh")
    bias = P(None, "zh")
    return jax.shard_map(
        local,
        mesh=fine,
        in_specs=(tokens, P("zh", None, None), last, last, rows, bias, rows, bias, rows, bias, rows, bias, tokens),
        out_specs=(tokens, tokens, last, last, rows, bias, rows, bias, rows, bias, rows, bias),
        check_vma=False,
    )
```

profile of v0, /device:TPU:1, one launch (start us, length us, event | category | flops | bytes accessed | tf_op | source)
XLA Modules:
  0.0 515.8 jit_solution(3316199432500222349)
XLA Ops:
  16.5 23.8 %collective-permute-done.refs_1_.refs_3_.refs_2_ = bf16[1376,384]{1,0:T(8,128)(2,1)S(1)} collective-permute-done((bf16[1376,384]{1,0:T(8,128)(2,1)}, bf16[1376,384]{1,0:T(8,128)(2,1)S(1)}, u32[]{:S(2)}, u32[]{:S(2)}) %collective-permute-start) | collective-permute-done | bytes 1056800 | tf_op jit(solution)/shard_map/ppermute | solution.py:1354
  53.8 6.0 %all-to-all-start = ((bf16[16,192,128]{2,1,0:T(8,128)(2,1)}), bf16[16,192,128]{2,1,0:T(8,128)(2,1)S(1)}, u32[]{:S(2)}, u32[]{:S(2)}) async-start(bf16[16,192,128]{2,1,0:T(8,128)(2,1)} %bitcast.56), calls=%async_computation | async-start | bytes 1572864 | tf_op jit(solution)/shard_map/all_to_all | solution.py:1338
  66.2 7.2 %all-to-all-done.refs_2_.refs_0_ = bf16[16,192,128]{2,1,0:T(8,128)(2,1)S(1)} async-done(((bf16[16,192,128]{2,1,0:T(8,128)(2,1)}), bf16[16,192,128]{2,1,0:T(8,128)(2,1)S(1)}, u32[]{:S(2)}, u32[]{:S(2)}) %all-to-all-start) | async-done | bytes 786464 | tf_op jit(solution)/shard_map/all_to_all | solution.py:1338
  86.1 8.1 %attention_forward.1 = (bf16[16,64,128]{2,1,0:T(8,128)(2,1)}, f32[64,2048]{1,0:T(8,128)}, f32[1,2048]{1,0:T(1,128)}) custom-call(s32[9]{0:T(128)} %stack.39.at, bf16[16,192,128]{2,1,0:T(8,128)(2,1)} %copy-done.2, bf16[128,128]{1,0:T(8,128)(2,1)} %copy-done.35, s32[1,2048]{1,0:T(1,128)} %fusion.1.refs_2_, s32[1,2048]{1,0:T(1,128)} %bitcast.66, ...), custom_call_target="tpu_custom_call" | custom-call | flops 1 | bytes 1 | tf_op jit(solution)/shard_map/attention_forward/pallas_call | solution.py:90
  105.7 7.1 %mlp.2 = (bf16[256,1536]{1,0:T(8,128)(2,1)}, f32[256,1536]{1,0:T(8,128)}, f32[256,768]{1,0:T(8,128)}) custom-call(s32[9]{0:T(128)} %stack.39.at, bf16[128,1536]{1,0:T(8,128)(2,1)} %get-tuple-element.119.refs_0_.refs_1_, bf16[128,1536]{1,0:T(8,128)(2,1)} %copy-done.5, f32[1,1536]{1,0:T(1,128)} %get-tuple-element.127.refs_2_, bf16[2,384,3072]{2,1,0:T(8,128)(2,1)} %refs_4_.9, ...), custom_call_target="tpu_custom_call" | custom-call | flops 1 | bytes 1 | tf_op jit(solution)/shard_map/mlp/pallas_call | solution.py:90
  141.6 7.0 %mlp.3 = (bf16[256,1536]{1,0:T(8,128)(2,1)}, f32[256,1536]{1,0:T(8,128)}, f32[256,768]{1,0:T(8,128)}) custom-call(s32[9]{0:T(128)} %stack.39.at, bf16[128,1536]{1,0:T(8,128)(2,1)} %get-tuple-element.136.refs_0_.refs_8_.refs_1_, bf16[128,1536]{1,0:T(8,128)(2,1)} %copy-done.6, f32[1,1536]{1,0:T(1,128)} %get-tuple-element.140.refs_2_, ...), custom_call_target="tpu_custom_call" | custom-call | flops 1 | bytes 1 | tf_op jit(solution)/shard_map/mlp/pallas_call | solution.py:90
  148.7 7.8 %mlp_back.2 = (bf16[256,1536]{1,0:T(8,128)(2,1)}, f32[128,768]{1,0:T(8,128)}, f32[128,768]{1,0:T(8,128)}, f32[4,384]{1,0:T(4,128)}, bf16[256,3456]{1,0:T(8,128)(2,1)}) custom-call(s32[9]{0:T(128)} %stack.39.at, bf16[128,768]{1,0:T(8,128)(2,1)} %bitcast.58, bf16[128,768]{1,0:T(8,128)(2,1)} %copy-done.12, f32[256,1536]{1,0:T(8,128)} %get-tuple-element.142.refs_2_, ...), custom_call_target="tpu_custom_call" | custom-call | flops 1 | bytes 1 | tf_op jit(solution)/shard_map/mlp_back/pallas_call | solution.py:90
  168.1 13.3 %attention_forward_backward.1 = (bf16[16,256,128]{2,1,0:T(8,128)(2,1)}, f32[128,128]{1,0:T(8,128)}, f32[128,128]{1,0:T(8,128)}) custom-call(s32[9]{0:T(128)} %stack.39.at, bf16[16,256,128]{2,1,0:T(8,128)(2,1)} %copy-done.7, bf16[128,128]{1,0:T(8,128)(2,1)} %copy-done.44, s32[1,2048]{1,0:T(1,128)} %fusion.1.refs_2_, s32[1,2048]{1,0:T(1,128)} %bitcast.67, ...), custom_call_target="tpu_custom_call" | custom-call | flops 1 | bytes 1 | tf_op jit(solution)/shard_map/attention_forward_backward/pallas_call | solution.py:90
  193.3 7.0 %collective-permute-done.10.refs_6_ = bf16[256,3456]{1,0:T(8,128)(2,1)S(1)} collective-permute-done((bf16[256,3456]{1,0:T(8,128)(2,1)}, bf16[256,3456]{1,0:T(8,128)(2,1)S(1)}, u32[]{:S(2)}, u32[]{:S(2)}) %collective-permute-start.10) | collective-permute-done | bytes 1769504 | tf_op jit(solution)/shard_map/ppermute | solution.py:1385
  201.5 6.5 %own_grads.2 = (bf16[16,192,384]{2,1,0:T(8,128)(2,1)}, f32[8,128]{1,0:T(8,128)}) custom-call(s32[9]{0:T(128)} %stack.39.at, bf16[128,1536]{1,0:T(8,128)(2,1)} %get-tuple-element.136.refs_0_.refs_8_.refs_1_, bf16[128,1536]{1,0:T(8,128)(2,1)} %copy-done.6, bf16[128,768]{1,0:T(8,128)(2,1)} %bitcast.59, bf16[128,768]{1,0:T(8,128)(2,1)} %copy-done.12, ...), custom_call_target="tpu_custom_call" | custom-call | flops 1 | bytes 1 | tf_op jit(solution)/shard_map/own_grads/pallas_call | solution.py:90
  210.4 11.8 %collective-permute-start.12 = (f32[128,768]{1,0:T(8,128)S(1)}, f32[128,768]{1,0:T(8,128)S(1)}, u32[]{:S(2)}, u32[]{:S(2)}) collective-permute-start(f32[128,768]{1,0:T(8,128)S(1)} %copy-done.49), channel_id=1, source_target_pairs={{0,2},{2,0},{1,3},{3,1},{4,6},{6,4},{5,7},{7,5},{8,10},{10,8},{9,1... | collective-permute-start | bytes 1179656 | tf_op jit(solution)/shard_map/ppermute | solution.py:1209
  246.2 7.5 %mlp_back.3 = (bf16[256,1536]{1,0:T(8,128)(2,1)}, f32[128,768]{1,0:T(8,128)}, f32[128,768]{1,0:T(8,128)}, f32[4,384]{1,0:T(4,128)}, bf16[256,2304]{1,0:T(8,128)(2,1)}) custom-call(s32[9]{0:T(128)} %stack.39.at, bf16[128,768]{1,0:T(8,128)(2,1)} %get-tuple-element.163.refs_0_.refs_2_, bf16[128,768]{1,0:T(8,128)(2,1)} %copy-done.16, ...), custom_call_target="tpu_custom_call" | custom-call | flops 1 | bytes 1 | tf_op jit(solution)/shard_map/mlp_back/pallas_call | solution.py:90
  264.1 9.6 %attention_backward.1 = (bf16[16,192,128]{2,1,0:T(8,128)(2,1)}, f32[128,128]{1,0:T(8,128)}, f32[128,128]{1,0:T(8,128)}) custom-call(s32[9]{0:T(128)} %stack.39.at, bf16[16,192,128]{2,1,0:T(8,128)(2,1)} %copy-done.2, bf16[128,128]{1,0:T(8,128)(2,1)} %copy-done.35, s32[1,2048]{1,0:T(1,128)} %fusion.1.refs_2_, s32[1,2048]{1,0:T(1,128)} %bitcast.68, ...), custom_call_target="tpu_custom_call" | custom-call | flops 1 | bytes 1 | tf_op jit(solution)/shard_map/attention_backward/pallas_call | solution.py:90
  292.2 7.4 %own_grads.3 = (bf16[16,224,384]{2,1,0:T(8,128)(2,1)}, f32[8,128]{1,0:T(8,128)}) custom-call(s32[9]{0:T(128)} %stack.39.at, bf16[128,1536]{1,0:T(8,128)(2,1)} %get-tuple-element.119.refs_0_.refs_1_, bf16[128,1536]{1,0:T(8,128)(2,1)} %copy-done.5, bf16[128,768]{1,0:T(8,128)(2,1)} %get-tuple-element.163.refs_0_.refs_2_, bf16[128,768]{1,0:T(8,128)(2,1)} %copy-done.16, ...), custom_call_target="tpu_custom_call" | custom-call | flops 1 | bytes 1 | tf_op jit(solution)/shard_map/own_grads/pallas_call | solution.py:90
  307.0 7.0 %collective-permute-start.18 = (f32[128,768]{1,0:T(8,128)S(1)}, f32[128,768]{1,0:T(8,128)S(1)}, u32[]{:S(2)}, u32[]{:S(2)}) collective-permute-start(f32[128,768]{1,0:T(8,128)S(1)} %copy-done.48), channel_id=1, source_target_pairs={{0,2},{2,0},{1,3},{3,1},{4,6},{6,4},{5,7},{7,5},{8,10},{10,8},{9,1... | collective-permute-start | bytes 1179656 | tf_op jit(solution)/shard_map/ppermute | solution.py:1209
  326.0 17.1 %all-to-all-done.6 = bf16[16,224,384]{2,1,0:T(8,128)(2,1)S(1)} async-done(((bf16[16,224,384]{2,1,0:T(8,128)(2,1)}), bf16[16,224,384]{2,1,0:T(8,128)(2,1)S(1)}, u32[]{:S(2)}, u32[]{:S(2)}) %all-to-all-start.6) | async-done | bytes 2752544 | tf_op jit(solution)/shard_map/all_to_all | solution.py:1245
  364.1 7.6 %all-to-all-start.7 = ((bf16[64,40,384]{2,1,0:T(8,128)(2,1)}), bf16[64,40,384]{2,1,0:T(8,128)(2,1)S(1)}, u32[]{:S(2)}, u32[]{:S(2)}) async-start(bf16[64,40,384]{2,1,0:T(8,128)(2,1)} %bitcast.31), calls=%async_computation.10 | async-start | bytes 3932160 | tf_op jit(solution)/shard_map/all_to_all | solution.py:1214
  376.3 6.7 %collective-permute-done.21 = bf16[224,384]{1,0:T(8,128)(2,1)S(1)} collective-permute-done((bf16[224,384]{1,0:T(8,128)(2,1)S(1)}, bf16[224,384]{1,0:T(8,128)(2,1)S(1)}, u32[]{:S(2)}, u32[]{:S(2)}) %collective-permute-start.21) | collective-permute-done | bytes 172064 | tf_op jit(solution)/shard_map/ppermute | solution.py:1250
  383.0 15.4 %collective-permute-done.25 = bf16[96,384]{1,0:T(8,128)(2,1)S(1)} collective-permute-done((bf16[96,384]{1,0:T(8,128)(2,1)S(1)}, bf16[96,384]{1,0:T(8,128)(2,1)S(1)}, u32[]{:S(2)}, u32[]{:S(2)}) %collective-permute-start.25) | collective-permute-done | bytes 73760 | tf_op jit(solution)/shard_map/ppermute | solution.py:1257
  441.6 8.1 %collective-permute-done.36.refs_7_ = bf16[640,384]{1,0:T(8,128)(2,1)} collective-permute-done((bf16[640,384]{1,0:T(8,128)(2,1)}, bf16[640,384]{1,0:T(8,128)(2,1)}, u32[]{:S(2)}, u32[]{:S(2)}) %collective-permute-start.36) | collective-permute-done | bytes 491552 | tf_op jit(solution)/shard_map/ppermute | solution.py:1223
  453.0 7.4 %place_second.1 = (f32[2,384,3072]{2,1,0:T(8,128)}, f32[2,1536,768]{2,1,0:T(8,128)}, f32[8,128]{1,0:T(8,128)}) custom-call(s32[9]{0:T(128)} %stack.39.at, bf16[3072,384]{1,0:T(8,128)(2,1)} %get-tuple-element.204.refs_0_, bf16[3072,384]{1,0:T(8,128)(2,1)} %copy-done.14, f32[8,128]{1,0:T(8,128)} %get-tuple-element.205.refs_2_), custom_call_target="tpu_custom_call" | custom-call | flops 1 | bytes 1 | tf_op jit(solution)/shard_map/place_second/pallas_call | solution.py:90
  460.9 10.6 %collective-permute-done.34.refs_5_ = bf16[640,384]{1,0:T(8,128)(2,1)} collective-permute-done((bf16[640,384]{1,0:T(8,128)(2,1)}, bf16[640,384]{1,0:T(8,128)(2,1)}, u32[]{:S(2)}, u32[]{:S(2)}) %collective-permute-start.34) | collective-permute-done | bytes 491552 | tf_op jit(solution)/shard_map/ppermute | solution.py:1223
  482.9 6.8 %collective-permute-done.19 = f32[128,768]{1,0:T(8,128)S(1)} collective-permute-done((f32[128,768]{1,0:T(8,128)S(1)}, f32[128,768]{1,0:T(8,128)S(1)}, u32[]{:S(2)}, u32[]{:S(2)}) %collective-permute-start.19) | collective-permute-done | bytes 393248 | tf_op jit(solution)/shard_map/ppermute | solution.py:1209
  497.1 11.7 %place_first.1 = (f32[2,384,3072]{2,1,0:T(8,128)}, f32[2,1536,768]{2,1,0:T(8,128)}, f32[2,384,768]{2,1,0:T(8,128)}, f32[2,384,2304]{2,1,0:T(8,128)}, f32[8,128]{1,0:T(8,128)}) custom-call(s32[9]{0:T(128)} %stack.39.at, bf16[5120,384]{1,0:T(8,128)(2,1)} %ring_collect.1.refs_2_.refs_0_, ...), custom_call_target="tpu_custom_call", output_to_operand_aliasing={{0}: (3, {}), {1}: (4, {}), {3}: (5, {})} | custom-call | flops 1 | bytes 1 | tf_op jit(solution)/shard_map/place_first/pallas_call | solution.py:90
  (275 shorter events, 272.5 us)
Async XLA Ops:
  7.2 98.6 %all-gather.4.cloned.1.call-start = ((), (), s32[]{:S(2)}) async-start(), calls=%async_computation.13 | async-start | bytes 2506752 | tf_op jit(solution)/shard_map/all_gather | solution.py:1351
  12.1 28.2 %collective-permute-start = (bf16[1376,384]{1,0:T(8,128)(2,1)}, bf16[1376,384]{1,0:T(8,128)(2,1)S(1)}, u32[]{:S(2)}, u32[]{:S(2)}) collective-permute-start(bf16[1376,384]{1,0:T(8,128)(2,1)} %begin.1.refs_0_.refs_2_.refs_1_), channel_id=1, source_target_pairs={{0,1},{1,0},{2,3},{3,2},{4,5},{5,4},{6,7},{7,6},{8,9},{9,8},{10,11... | collective-permute-start | bytes 3170312 | tf_op jit(solution)/shard_map/ppermute | solution.py:1354
  59.7 81.9 %all-gather.6.cloned.1.call-start = ((), (), s32[]{:S(2)}) async-start(), calls=%async_computation.14 | async-start | bytes 2506752 | tf_op jit(solution)/shard_map/all_gather | solution.py:1351
  102.7 25.3 %collective-permute-start.7 = (bf16[1152,384]{1,0:T(8,128)(2,1)}, bf16[1152,384]{1,0:T(8,128)(2,1)S(1)}, u32[]{:S(2)}, u32[]{:S(2)}) collective-permute-start(bf16[1152,384]{1,0:T(8,128)(2,1)} %get-tuple-element.137.refs_2_.refs_1_), channel_id=1, source_target_pairs={{0,1},{1,0},{2,3},{3,2},{4,5},{5,4},{6,7},{7,6},{8,9},{9,8},{10,11... | collective-permute-start | bytes 2654216 | tf_op jit(solution)/shard_map/ppermute | solution.py:1366
  133.5 23.0 %all-to-all-start.2 = ((bf16[16,256,128]{2,1,0:T(8,128)(2,1)}), bf16[16,256,128]{2,1,0:T(8,128)(2,1)S(1)}, u32[]{:S(2)}, u32[]{:S(2)}) async-start(bf16[16,256,128]{2,1,0:T(8,128)(2,1)} %bitcast.52), calls=%async_computation.2 | async-start | bytes 2097152 | tf_op jit(solution)/shard_map/all_to_all | solution.py:1338
  158.7 41.5 %collective-permute-start.10 = (bf16[256,3456]{1,0:T(8,128)(2,1)}, bf16[256,3456]{1,0:T(8,128)(2,1)S(1)}, u32[]{:S(2)}, u32[]{:S(2)}) collective-permute-start(bf16[256,3456]{1,0:T(8,128)(2,1)} %get-tuple-element.152), channel_id=1, source_target_pairs={{0,1},{1,0},{2,3},{3,2},{4,5},{5,4},{6,7},{7,6},{8,9},{9,8},{10,11... | collective-permute-start | bytes 5308424 | tf_op jit(solution)/shard_map/ppermute | solution.py:1385
  193.1 65.9 %reduce-scatter.5.cloned.1.call-start = ((), (), s32[]{:S(2)}) async-start(), calls=%async_computation.15 | async-start | bytes 2949120 | tf_op jit(solution)/shard_map/reduce_scatter | solution.py:1237
  229.6 29.4 %collective-permute-start.14 = (bf16[256,1408]{1,0:T(8,128)(2,1)}, bf16[256,1408]{1,0:T(8,128)(2,1)S(1)}, u32[]{:S(2)}, u32[]{:S(2)}) collective-permute-start(bf16[256,1408]{1,0:T(8,128)(2,1)} %pack_early.1.refs_8_), channel_id=1, source_target_pairs={{0,1},{1,0},{2,3},{3,2},{4,5},{5,4},{6,7},{7,6},{8,9},{9,8},{10,11... | collective-permute-start | bytes 2162696 | tf_op jit(solution)/shard_map/ppermute | solution.py:1393
  246.1 78.3 %reduce-scatter.9.cloned.1.call-start = ((), (), s32[]{:S(2)}) async-start(), calls=%async_computation.17 | async-start | bytes 737280 | tf_op jit(solution)/shard_map/reduce_scatter | solution.py:1241
  261.2 63.2 %reduce-scatter.7.cloned.1.call-start = ((), (), s32[]{:S(2)}) async-start(), calls=%async_computation.16 | async-start | bytes 2949120 | tf_op jit(solution)/shard_map/reduce_scatter | solution.py:1237
  262.4 28.7 %collective-permute-start.16 = (bf16[256,2304]{1,0:T(8,128)(2,1)S(1)}, bf16[256,2304]{1,0:T(8,128)(2,1)S(1)}, u32[]{:S(2)}, u32[]{:S(2)}) collective-permute-start(bf16[256,2304]{1,0:T(8,128)(2,1)S(1)} %copy-done.21), channel_id=1, source_target_pairs={{0,1},{1,0},{2,3},{3,2},{4,5},{5,4},{6,7},{7,6},{8,9},{9,8},{10,11... | collective-permute-start | bytes 3538952 | tf_op jit(solution)/shard_map/ppermute | solution.py:1402
  301.7 41.4 %all-to-all-start.6 = ((bf16[16,224,384]{2,1,0:T(8,128)(2,1)}), bf16[16,224,384]{2,1,0:T(8,128)(2,1)S(1)}, u32[]{:S(2)}, u32[]{:S(2)}) async-start(bf16[16,224,384]{2,1,0:T(8,128)(2,1)} %get-tuple-element.189), calls=%async_computation.7 | async-start | bytes 5505024 | tf_op jit(solution)/shard_map/all_to_all | solution.py:1245
  307.0 49.7 %reduce-scatter.11.cloned.1.call-start = ((), (), s32[]{:S(2)}) async-start(), calls=%async_computation.18 | async-start | bytes 737280 | tf_op jit(solution)/shard_map/reduce_scatter | solution.py:1241
  325.7 101.0 %all-gather.8.cloned.1.call-start = ((), (), s32[]{:S(2)}) async-start(), calls=%async_computation.19 | async-start | bytes 2506752 | tf_op jit(solution)/shard_map/all_gather | solution.py:1420
  364.1 45.2 %all-to-all-start.7 = ((bf16[64,40,384]{2,1,0:T(8,128)(2,1)}), bf16[64,40,384]{2,1,0:T(8,128)(2,1)S(1)}, u32[]{:S(2)}, u32[]{:S(2)}) async-start(bf16[64,40,384]{2,1,0:T(8,128)(2,1)} %bitcast.31), calls=%async_computation.10 | async-start | bytes 3932160 | tf_op jit(solution)/shard_map/all_to_all | solution.py:1214
  372.9 25.5 %collective-permute-start.27 = (bf16[96,384]{1,0:T(8,128)(2,1)S(1)}, bf16[96,384]{1,0:T(8,128)(2,1)S(1)}, u32[]{:S(2)}, u32[]{:S(2)}) collective-permute-start(bf16[96,384]{1,0:T(8,128)(2,1)S(1)} %get-tuple-element.223), channel_id=1, source_target_pairs={{0,17},{17,0},{1,16},{16,1},{2,19},{19,2},{3,18},{18,3},{4,21},{21... | collective-permute-start | bytes 221192 | tf_op jit(solution)/shard_map/ppermute | solution.py:1259
  374.9 23.5 %collective-permute-start.26 = (bf16[96,384]{1,0:T(8,128)(2,1)S(1)}, bf16[96,384]{1,0:T(8,128)(2,1)S(1)}, u32[]{:S(2)}, u32[]{:S(2)}) collective-permute-start(bf16[96,384]{1,0:T(8,128)(2,1)S(1)} %get-tuple-element.223), channel_id=1, source_target_pairs={{0,1},{1,0},{2,3},{3,2},{4,5},{5,4},{6,7},{7,6},{8,9},{9,8},{10,11... | collective-permute-start | bytes 221192 | tf_op jit(solution)/shard_map/ppermute | solution.py:1258
  375.6 22.8 %collective-permute-start.25 = (bf16[96,384]{1,0:T(8,128)(2,1)S(1)}, bf16[96,384]{1,0:T(8,128)(2,1)S(1)}, u32[]{:S(2)}, u32[]{:S(2)}) collective-permute-start(bf16[96,384]{1,0:T(8,128)(2,1)S(1)} %get-tuple-element.222), channel_id=1, source_target_pairs={{0,16},{16,0},{1,17},{17,1},{2,18},{18,2},{3,19},{19,3},{4,20},{20... | collective-permute-start | bytes 221192 | tf_op jit(solution)/shard_map/ppermute | solution.py:1257
  427.9 23.7 %collective-permute-start.38 = (bf16[3072,384]{1,0:T(8,128)(2,1)}, bf16[3072,384]{1,0:T(8,128)(2,1)S(1)}, u32[]{:S(2)}, u32[]{:S(2)}) collective-permute-start(bf16[3072,384]{1,0:T(8,128)(2,1)} %get-tuple-element.204.refs_0_), channel_id=1, source_target_pairs={{0,2},{2,0},{1,3},{3,1},{4,6},{6,4},{5,7},{7,5},{8,10},{10,8},{9,1... | collective-permute-start | bytes 7077896 | tf_op jit(solution)/shard_map/ppermute | solution.py:1209
  430.8 44.4 %all-to-all-start.8 = ((bf16[32,40,384]{2,1,0:T(8,128)(2,1)}), bf16[32,40,384]{2,1,0:T(8,128)(2,1)S(1)}, u32[]{:S(2)}, u32[]{:S(2)}) async-start(bf16[32,40,384]{2,1,0:T(8,128)(2,1)} %broadcast_in_dim.60), calls=%async_computation.11 | async-start | bytes 1966080 | tf_op jit(solution)/shard_map/all_to_all | solution.py:1276
  436.1 24.8 %collective-permute-start.35 = (bf16[640,384]{1,0:T(8,128)(2,1)}, bf16[640,384]{1,0:T(8,128)(2,1)S(1)}, u32[]{:S(2)}, u32[]{:S(2)}) collective-permute-start(bf16[640,384]{1,0:T(8,128)(2,1)} %get-tuple-element.202.refs_4_), channel_id=1, source_target_pairs={{0,8},{4,12},{8,0},{12,4},{1,9},{5,13},{9,1},{13,5},{2,10},{6,14},... | collective-permute-start | bytes 1474568 | tf_op jit(solution)/shard_map/ppermute | solution.py:1223
  438.9 32.6 %collective-permute-start.34 = (bf16[640,384]{1,0:T(8,128)(2,1)}, bf16[640,384]{1,0:T(8,128)(2,1)}, u32[]{:S(2)}, u32[]{:S(2)}) collective-permute-start(bf16[640,384]{1,0:T(8,128)(2,1)} %get-tuple-element.202.refs_4_), channel_id=1, source_target_pairs={{0,4},{4,8},{8,12},{12,0},{1,5},{5,9},{9,13},{13,1},{2,6},{6,10},{... | collective-permute-start | bytes 1474568 | tf_op jit(solution)/shard_map/ppermute | solution.py:1223
  439.2 32.3 %collective-permute-start.33 = (bf16[640,384]{1,0:T(8,128)(2,1)}, bf16[640,384]{1,0:T(8,128)(2,1)}, u32[]{:S(2)}, u32[]{:S(2)}) collective-permute-start(bf16[640,384]{1,0:T(8,128)(2,1)} %get-tuple-element.201.refs_1_.refs_0_), channel_id=1, source_target_pairs={{0,96},{32,0},{64,32},{96,64},{1,97},{33,1},{65,33},{97,65},{2,98}... | collective-permute-start | bytes 1474568 | tf_op jit(solution)/shard_map/ppermute | solution.py:1223
  451.6 23.6 %collective-permute-start.31 = (bf16[640,384]{1,0:T(8,128)(2,1)}, bf16[640,384]{1,0:T(8,128)(2,1)}, u32[]{:S(2)}, u32[]{:S(2)}) collective-permute-start(bf16[640,384]{1,0:T(8,128)(2,1)} %get-tuple-element.201.refs_1_.refs_0_), channel_id=1, source_target_pairs={{0,32},{32,64},{64,96},{96,0},{1,33},{33,65},{65,97},{97,1},{2,34}... | collective-permute-start | bytes 1474568 | tf_op jit(solution)/shard_map/ppermute | solution.py:1223
  (82 other events, 624.9 us)
Sparse Core Ops, SparseCore 0:
  41.1 50.6 all-gather.3
  96.9 44.6 all-gather.5
  210.5 42.1 reduce-scatter.4
  261.3 19.7 reduce-scatter.8
  283.9 39.5 reduce-scatter.6
  325.8 30.8 reduce-scatter.10
  364.2 62.3 all-gather.7
where the time goes:
time: 526 us; the launch traced here: 516 us
  Pallas kernels  189 us (36%)
  waiting for transfers between devices  151 us (29%)
  starting transfers between devices  125 us (24%)
  local copies, waits for them, and re-layouts  26.9 us (5%)
  between operations  14.8 us (3%)
  other arithmetic  8.46 us (2%)
    pallas_call x43, Pallas kernels, run(): pl.pallas_call(body, grid_spec=pltpu.PrefetchScalarGridSpec(num_scalar_pr...  189 us
    ppermute x12, waiting for transfers between devices, ring(): lax.ppermute(values, axis, [(place, (place + by) % 4) for place in range(...  31.3 us
    all_to_all x6, starting transfers between devices, to_units(): lax.all_to_all(values.reshape(TILES, -1, TILE), CHIPS, 0, 0, tiled=True)  27.9 us
    ppermute x13, starting transfers between devices, exchange(): return lax.ppermute(values, 'core', SWAP)  26.3 us
    ppermute x1, waiting for transfers between devices, local(): own_qkv, other_qkv = ([weights], [lax.ppermute(weights, 'zh', SWAP)])  23.8 us
    unnamed x101, local copies, waits for them, and re-layouts  21.6 us
    ppermute x12, starting transfers between devices, ring(): lax.ppermute(values, axis, [(place, (place + by) % 4) for place in range(...  19.2 us
    all_to_all x1, waiting for transfers between devices, sum_grid(): parts = lax.all_to_all(grads, ACROSS, 0, 0, tiled=True)  17.1 us
  transfers between devices with their start and end apart: 56, of which 30 were waited for; matrix products, arithmetic and copies ran while one was open for 2% of the time, Pallas kernels for 31%

commit v1 on v0

--- a/solution.py
+++ b/solution.py
@@ -814,41 +814,6 @@
     )[0]
 
 
-def spread_kernel(at, *refs):
-    outs = refs[8:]
-    rows = outs[0].shape[0] // 4
-    for index, axis in ((0, RING_Y), (1, RING_X)):
-        for step in range(4):
-            place = (at[axis] + 4 - step) % 4
-            outs[index][pl.ds(pl.multiple_of(place * rows, 32), rows), :] = refs[4 * index + step][...]
-
-
-def spread(at, pieces, after):
-    rows = pieces[0].shape[0]
-    outs = [shape((4 * rows, HALF), BF16)] * 2
-    return run(spread_kernel, at, pieces, outs, "ring_spread", 0, 32 * rows * HALF, after=after)
-
-
-def collect_kernel(at, *refs):
-    out_ref = refs[8]
-    rows = refs[0].shape[0] // 4
-    for step in range(4):
-        x = (at[RING_X] + 4 - step) % 4
-        for y in range(4):
-            to = pl.ds(pl.multiple_of((x * 4 + y) * 2 * rows, 32), rows)
-            out_ref[to, :] = refs[step][y * rows : (y + 1) * rows, :]
-        y = (at[RING_Y] + 4 - step) % 4
-        for x in range(4):
-            to = pl.ds(pl.multiple_of((x * 4 + y) * 2 * rows + rows, 32), rows)
-            out_ref[to, :] = refs[4 + step][x * rows : (x + 1) * rows, :]
-
-
-def collect(at, pieces, after):
-    rows = pieces[0].shape[0]
-    outs = [shape((8 * rows, HALF), BF16)]
-    return run(collect_kernel, at, pieces, outs, "ring_collect", 0, 32 * rows * HALF, after=after)[0]
-
-
 def qkv_back_kernel(at, got_ref, own_ref, other_ref, keep_ref, give_ref, bias_ref):
     z = at[ZH]
     rows = TILE // 2
@@ -977,16 +942,16 @@
         at += step
 
 
-def place_mlp(source, core, up_ref, down_ref, chunk, length):
+def place_mlp(source, core, up_ref, down_ref, chunk, length, offset=0):
     for part in range(4):
         z, side = part // 2, part % 2
         column = z * CORE_FF + core * QUARTER + side * HALF
-        for source_row, row, count in rows_of(part, 0, HALF, chunk, length):
+        for source_row, row, count in rows_of(part, 0, HALF, chunk, length, offset):
             up_ref[0, row : row + count, column : column + HALF] = source[source_row : source_row + count, :].astype(F32)
         side, index = part // 2, part % 2
         lanes = slice(side * HALF, (side + 1) * HALF)
         first = core * QUARTER + index * HALF
-        for source_row, row, count in rows_of(part, HALF, HALF, chunk, length):
+        for source_row, row, count in rows_of(part, HALF, HALF, chunk, length, offset):
             row += first
             down_ref[0, row : row + count, lanes] = source[source_row : source_row + count, :].astype(F32)
 
@@ -1016,81 +981,61 @@
     out_ref[0, :, column : column + HALF] = rows_ref[...].T
 
 
-def place_second_kernel(at, mine_ref, theirs_ref, up_ref, down_ref, done_ref):
-    done_ref[...] = jnp.zeros_like(done_ref)
-    for_cores(
-        at,
-        mine_ref,
-        theirs_ref,
-        lambda core, source: place_mlp(source, core, up_ref, down_ref, CHUNK_SECOND, CHUNK_SECOND),
-    )
-
-
-def place_second(at, mine, theirs):
-    outs = PLACED[:2]
-    return run(
-        place_second_kernel,
-        at,
-        [mine, theirs],
-        [shape(dims, F32) for dims in outs] + [shape((8, 128), F32)],
-        "place_second",
-        0,
-        14000000,
-        out_specs=[block((1,) + dims[1:], lambda s: (1, 0, 0)) for dims in outs] + [block((8, 128))],
-        token=True,
-    )[:-1]
-
-
-def place_first_kernel(
-    at, mine_ref, theirs_ref, up_in, down_in, qkv_in, up_ref, down_ref, out_ref, qkv_ref, done_ref, rows_ref
-):
-    length = CHUNK_FIRST + CHUNK_QKV
-    done_ref[...] = jnp.zeros_like(done_ref)
-
-    def put(core, source):
-        place_mlp(source, core, up_ref, down_ref, CHUNK_FIRST, length)
-        place_out(source, core, out_ref.at[0:1], 2 * HALF, CHUNK_FIRST, length, 0)
-        place_out(source, core, out_ref.at[1:2], QKV_PART, CHUNK_QKV, length, CHUNK_FIRST)
-
-    for_cores(at, mine_ref, theirs_ref, put)
-    for part in range(3):
-        for z in range(2):
-
-            def put_rows(core, source):
-                for head in range(3):
-                    row = (z * 3 + head) * QKV + part * HEAD
-                    to = core * QKV + head * HEAD
-                    for first in range(row, row + HEAD, 32):
-                        pieces = rows_of(first // QKV_PART, first % QKV_PART, 32, CHUNK_QKV, length, CHUNK_FIRST)
-                        for source_row, more, count in pieces:
-                            here = to + first - row + more
-                            rows_ref[here : here + count, :] = source[source_row : source_row + count, :].astype(F32)
-
-            for_cores(at, mine_ref, theirs_ref, put_rows)
-            place_turned(rows_ref, qkv_ref, part, z)
-
-
-def place_first(at, mine, theirs, up, down, qkv):
+LENGTH = CHUNK_FIRST + CHUNK_QKV + CHUNK_SECOND
+
+
+def place_long_kernel(at, mine_ref, theirs_ref, qkv_in, token, up_ref, down_ref, out_ref, qkv_ref, rows_ref):
+    def first(core, source):
+        place_mlp(source, core, up_ref, down_ref, CHUNK_FIRST, LENGTH)
+        place_out(source, core, out_ref, 2 * HALF, CHUNK_FIRST, LENGTH, 0)
+
+    def second(core, source):
+        place_mlp(source, core, up_ref, down_ref, CHUNK_SECOND, LENGTH, CHUNK_FIRST + CHUNK_QKV)
+        place_out(source, core, out_ref, QKV_PART, CHUNK_QKV, LENGTH, CHUNK_FIRST)
+
+    @pl.when(pl.program_id(0) == 0)
+    def _():
+        for_cores(at, mine_ref, theirs_ref, first)
+        for part in range(3):
+            for z in range(2):
+
+                def put_rows(core, source):
+                    for head in range(3):
+                        row = (z * 3 + head) * QKV + part * HEAD
+                        to = core * QKV + head * HEAD
+                        for start in range(row, row + HEAD, 32):
+                            pieces = rows_of(start // QKV_PART, start % QKV_PART, 32, CHUNK_QKV, LENGTH, CHUNK_FIRST)
+                            for source_row, more, count in pieces:
+                                here = to + start - row + more
+                                rows_ref[here : here + count, :] = source[source_row : source_row + count, :].astype(F32)
+
+                for_cores(at, mine_ref, theirs_ref, put_rows)
+                place_turned(rows_ref, qkv_ref, part, z)
+
+    @pl.when(pl.program_id(0) == 1)
+    def _():
+        for_cores(at, mine_ref, theirs_ref, second)
+
+
+def place_long(at, mine, theirs, qkv):
     anywhere = pl.BlockSpec(memory_space=pl.ANY)
-    return run(
-        place_first_kernel,
-        at,
-        [mine, theirs, (up, anywhere), (down, anywhere), (qkv, anywhere)],
-        [shape(dims, F32) for dims in (*PLACED, QKV_SHAPE)] + [shape((8, 128), F32)],
-        "place_first",
-        0,
-        24000000,
-        [pltpu.VMEM((HALF, HALF), F32)],
-        aliases={3: 0, 4: 1, 5: 3},
-        out_specs=[
-            block((1,) + UP_SHAPE[1:], lambda s: (0, 0, 0)),
-            block((1,) + DOWN_SHAPE[1:], lambda s: (0, 0, 0)),
-            block(OUT_SHAPE),
-            block((1,) + QKV_SHAPE[1:], lambda s: (1, 0, 0)),
-            block((8, 128)),
-        ],
-        token=True,
-    )[:-1]
+    once = pl.BlockSpec(mine.shape, lambda i, s: (0, 0), pipeline_mode=pl.Buffered(1))
+    return pl.pallas_call(
+        place_long_kernel,
+        grid_spec=pltpu.PrefetchScalarGridSpec(
+            num_scalar_prefetch=1,
+            grid=(LAYERS,),
+            in_specs=[once, once, anywhere, anywhere],
+            out_specs=[pl.BlockSpec((1,) + dims[1:], lambda i, s: (i, 0, 0)) for dims in PLACED]
+            + [pl.BlockSpec((1,) + QKV_SHAPE[1:], lambda i, s: (1, 0, 0))],
+            scratch_shapes=[pltpu.VMEM((HALF, HALF), F32)],
+        ),
+        out_shape=[shape(dims, F32) for dims in (*PLACED, QKV_SHAPE)],
+        input_output_aliases={3: 3},
+        compiler_params=pltpu.CompilerParams(vmem_limit_bytes=60 * 1024 * 1024),
+        cost_estimate=pl.CostEstimate(flops=1, bytes_accessed=1, transcendentals=0),
+        name="place_long",
+    )(at, mine, theirs, qkv, *LATEST)
 
 
 def place_qkv_kernel(
@@ -1259,16 +1204,6 @@
     across = lax.ppermute(give, ("zl", "zh"), [(0, 3), (3, 0), (1, 2), (2, 1)])
     total = (keep.astype(F32) + near.astype(F32)) + (far.astype(F32) + across.astype(F32))
     return total.astype(BF16)
-
-
-def gather_half(at, total, after):
-    rows = total.shape[0] // 2
-    halves = total[:rows], total[rows:]
-    return spread(at, around([halves[0]] * 4 + [halves[1]] * 4, Y_RING, X_RING), after)
-
-
-def gather_rest(at, long, after):
-    return collect(at, around([long[0]] * 4 + [long[1]] * 4, X_RING, Y_RING), after)
 
 
 def gather_short(part):
@@ -1377,7 +1312,7 @@
     stream, hat1, inverse1, act = norms(at, hidden_in[0], added, gain[1], offset[1])
     acts1 = (act, exchange(act))
     got1 = to_units(project_qkv(at, *acts1, own_qkv[1], other_qkv[1], b_qkv[1], *own_tables, dctx1))
-    gate1, slope1, total = feed_forward(at, *acts1, b_up[1], up_weight, down_weight, rest, 1)
+    gate1, slope1, mlp1 = feed_forward(at, *acts1, b_up[1], up_weight, down_weight, rest, 1)
     dup1, keep, give, sum_up1, sent = mlp_back(
         at, *dhid1, slope1, up_weight, down_weight, rest, 1, (*acts1, gate1)
     )
@@ -1415,18 +1350,16 @@
 
     sums = (sum_norm0, sum_up0, sum_qkv0, sum_norm1, sum_up1, sum_qkv1)
     part_qkv = scatter_sum(qkv_grads_first(at, dqkv0, *acts0, sums, (part0,)))
-    keep, give = attention_out(at, dqkv1, outs, total, 1)
-    partq, part1 = held(at, [partq, part1])
-    long1 = lax.all_gather(sum_near(part1), ACROSS, axis=0, tiled=True)
+    part0, partq, part1 = held(at, [part0, partq, part1])
+    total = [sum_near(part0), sum_depth(zh, partq), sum_near(part1)]
+    (total,) = held(at, [jnp.concatenate(total)])
+    long = lax.all_gather(total, ACROSS, axis=0, tiled=True)
+    keep, give = attention_out(at, dqkv1, outs, mlp1, 1, (part_qkv,))
     hidden_out = (stream + (keep + exchange(give) + b_rest[1])).astype(BF16)[None]
-    total0 = jnp.concatenate([sum_near(part0), sum_depth(zh, partq)])
-    half0 = gather_half(at, total0, (part_qkv,))
-    long1 = held(at, [long1])[0]
     qkv0 = gather_short(part_qkv)
-    g_up, g_down = place_second(at, long1, exchange(long1))
-    long0 = gather_rest(at, half0, (qkv0,))
     g_qkv, g_gain, g_offset, g_hidden, g_again, g_bqkv, g_bup = place_qkv(at, qkv0, exchange(qkv0))
-    g_up, g_down, g_out, g_qkv = place_first(at, long0, exchange(long0), g_up, g_down, g_qkv)
+    (long,) = held(at, [long])
+    g_up, g_down, g_out, g_qkv = place_long(at, long, exchange(long), g_qkv)
     return (
         hidden_out,
         hidden_grad,

time: 526 us -> 505 us (0.960)
  blocking collectives: 0 us -> 67.1 us
  waiting for transfers between devices: 151 us -> 105 us
  starting transfers between devices: 125 us -> 94.1 us
  Pallas kernels: 189 us -> 179 us
    all_to_all x0 -> x2, blocking collectives: none -> 67.1 us  [the longest x1 37.5 us: scatter_sum(): parts = lax.all_to_all(parts, EVERY, 0, 0, tiled=True)]
    ppermute x12 -> x0, waiting for transfers between devices: 31.3 us -> none  [ring(): lax.ppermute(values, axis, [(place, (place + by) % 4) for place in range(...]
    pallas_call x43 -> x40, Pallas kernels: 189 us -> 163 us  [run(): pl.pallas_call(body, grid_spec=pltpu.PrefetchScalarGridSpec(num_scalar_pr...]
    ppermute x12 -> x0, starting transfers between devices: 19.2 us -> none  [ring(): lax.ppermute(values, axis, [(place, (place + by) % 4) for place in range(...]
    pallas_call x0 -> x1, Pallas kernels: none -> 16 us  [place_long(): pl.pallas_call(place_long_kernel, grid_spec=pltpu.PrefetchScalarGridSpec(...]
    ppermute x1, waiting for transfers between devices: 15.4 us -> 0.01 us  [sum_depth(): near = lax.ppermute(keep, 'zl', SWAP)]
    all_to_all x2 -> x0, starting transfers between devices: 12.9 us -> none  [the longest x1 7.65 us: scatter_sum(): parts = lax.all_to_all(parts, EVERY, 0, 0, tiled=True)]
    ppermute x2, waiting for transfers between devices: 9.44 us -> 3.07 us  [sum_near(): return add_from(part, lax.ppermute(part, 'zl', SWAP))]
  transfers between devices with their start and end apart: 56 -> 41, of which waited for: 30 -> 25; matrix products, arithmetic and copies ran while one was open for 2% -> 3% of each run, Pallas kernels for 31% -> 31%
where the time goes in v1:
time: 505 us; the launch traced here: 495 us
  Pallas kernels  179 us (35%)
  waiting for transfers between devices  105 us (21%)
  starting transfers between devices  94.1 us (19%)
  blocking collectives  67.1 us (13%)
  local copies, waits for them, and re-layouts  23.3 us (5%)
  between operations  15 us (3%)
  other arithmetic  11.4 us (2%)
    pallas_call x40, Pallas kernels, run(): pl.pallas_call(body, grid_spec=pltpu.PrefetchScalarGridSpec(num_scalar_pr...  163 us
    all_to_all x1, blocking collectives, scatter_sum(): parts = lax.all_to_all(parts, EVERY, 0, 0, tiled=True)  37.5 us
    all_to_all x1, blocking collectives, gather_short(): return lax.all_to_all(copies, EVERY[1:], 0, 0, tiled=True).reshape(-1, HALF)  29.7 us
    ppermute x12, starting transfers between devices, exchange(): return lax.ppermute(values, 'core', SWAP)  28.6 us
    all_to_all x6, starting transfers between devices, to_units(): lax.all_to_all(values.reshape(TILES, -1, TILE), CHIPS, 0, 0, tiled=True)  27.9 us
    ppermute x1, waiting for transfers between devices, local(): own_qkv, other_qkv = ([weights], [lax.ppermute(weights, 'zh', SWAP)])  23.8 us
    unnamed x79, local copies, waits for them, and re-layouts  19 us
    all_to_all x1, waiting for transfers between devices, sum_grid(): parts = lax.all_to_all(grads, ACROSS, 0, 0, tiled=True)  17.1 us
  transfers between devices with their start and end apart: 41, of which 25 were waited for; matrix products, arithmetic and copies ran while one was open for 3% of the time, Pallas kernels for 31%

profile of v1, /device:TPU:1, one launch (start us, length us, event | category | flops | bytes accessed | tf_op | source)
XLA Modules:
  0.0 495.4 jit_solution(3579156648588060094)
XLA Ops:
  16.5 23.8 %collective-permute-done.refs_1_.refs_3_.refs_2_ = bf16[1376,384]{1,0:T(8,128)(2,1)S(1)} collective-permute-done((bf16[1376,384]{1,0:T(8,128)(2,1)}, bf16[1376,384]{1,0:T(8,128)(2,1)S(1)}, u32[]{:S(2)}, u32[]{:S(2)}) %collective-permute-start) | collective-permute-done | bytes 1056800 | tf_op jit(solution)/shard_map/ppermute | solution.py:1289
  53.8 5.9 %all-to-all-start = ((bf16[16,192,128]{2,1,0:T(8,128)(2,1)}), bf16[16,192,128]{2,1,0:T(8,128)(2,1)S(1)}, u32[]{:S(2)}, u32[]{:S(2)}) async-start(bf16[16,192,128]{2,1,0:T(8,128)(2,1)} %bitcast.54), calls=%async_computation | async-start | bytes 1572864 | tf_op jit(solution)/shard_map/all_to_all | solution.py:1273
  66.2 7.2 %all-to-all-done.refs_2_.refs_0_ = bf16[16,192,128]{2,1,0:T(8,128)(2,1)S(1)} async-done(((bf16[16,192,128]{2,1,0:T(8,128)(2,1)}), bf16[16,192,128]{2,1,0:T(8,128)(2,1)S(1)}, u32[]{:S(2)}, u32[]{:S(2)}) %all-to-all-start) | async-done | bytes 786464 | tf_op jit(solution)/shard_map/all_to_all | solution.py:1273
  86.1 8.1 %attention_forward.1 = (bf16[16,64,128]{2,1,0:T(8,128)(2,1)}, f32[64,2048]{1,0:T(8,128)}, f32[1,2048]{1,0:T(1,128)}) custom-call(s32[9]{0:T(128)} %stack.39.at, bf16[16,192,128]{2,1,0:T(8,128)(2,1)} %copy-done.3, bf16[128,128]{1,0:T(8,128)(2,1)} %copy-done.30, s32[1,2048]{1,0:T(1,128)} %fusion.1.refs_2_, s32[1,2048]{1,0:T(1,128)} %bitcast.66, ...), custom_call_target="tpu_custom_call" | custom-call | flops 1 | bytes 1 | tf_op jit(solution)/shard_map/attention_forward/pallas_call | solution.py:90
  105.7 7.1 %mlp.2 = (bf16[256,1536]{1,0:T(8,128)(2,1)}, f32[256,1536]{1,0:T(8,128)}, f32[256,768]{1,0:T(8,128)}) custom-call(s32[9]{0:T(128)} %stack.39.at, bf16[128,1536]{1,0:T(8,128)(2,1)} %get-tuple-element.117.refs_0_.refs_1_, bf16[128,1536]{1,0:T(8,128)(2,1)} %copy-done.6, f32[1,1536]{1,0:T(1,128)} %get-tuple-element.125.refs_2_, bf16[2,384,3072]{2,1,0:T(8,128)(2,1)} %refs_4_.9, ...), custom_call_target="tpu_custom_call" | custom-call | flops 1 | bytes 1 | tf_op jit(solution)/shard_map/mlp/pallas_call | solution.py:90
  133.4 5.7 %all-to-all-start.2 = ((bf16[16,256,128]{2,1,0:T(8,128)(2,1)}), bf16[16,256,128]{2,1,0:T(8,128)(2,1)S(1)}, u32[]{:S(2)}, u32[]{:S(2)}) async-start(bf16[16,256,128]{2,1,0:T(8,128)(2,1)} %bitcast.53), calls=%async_computation.2 | async-start | bytes 2097152 | tf_op jit(solution)/shard_map/all_to_all | solution.py:1273
  141.7 7.0 %mlp.3 = (bf16[256,1536]{1,0:T(8,128)(2,1)}, f32[256,1536]{1,0:T(8,128)}, f32[256,768]{1,0:T(8,128)}) custom-call(s32[9]{0:T(128)} %stack.39.at, bf16[128,1536]{1,0:T(8,128)(2,1)} %get-tuple-element.134.refs_0_.refs_8_.refs_1_, bf16[128,1536]{1,0:T(8,128)(2,1)} %copy-done.7, f32[1,1536]{1,0:T(1,128)} %get-tuple-element.138.refs_2_, ...), custom_call_target="tpu_custom_call" | custom-call | flops 1 | bytes 1 | tf_op jit(solution)/shard_map/mlp/pallas_call | solution.py:90
  148.7 7.8 %mlp_back.2 = (bf16[256,1536]{1,0:T(8,128)(2,1)}, f32[128,768]{1,0:T(8,128)}, f32[128,768]{1,0:T(8,128)}, f32[4,384]{1,0:T(4,128)}, bf16[256,3456]{1,0:T(8,128)(2,1)}) custom-call(s32[9]{0:T(128)} %stack.39.at, bf16[128,768]{1,0:T(8,128)(2,1)} %bitcast.56, bf16[128,768]{1,0:T(8,128)(2,1)} %copy-done.13, f32[256,1536]{1,0:T(8,128)} %get-tuple-element.140.refs_2_, ...), custom_call_target="tpu_custom_call" | custom-call | flops 1 | bytes 1 | tf_op jit(solution)/shard_map/mlp_back/pallas_call | solution.py:90
  168.0 13.3 %attention_forward_backward.1 = (bf16[16,256,128]{2,1,0:T(8,128)(2,1)}, f32[128,128]{1,0:T(8,128)}, f32[128,128]{1,0:T(8,128)}) custom-call(s32[9]{0:T(128)} %stack.39.at, bf16[16,256,128]{2,1,0:T(8,128)(2,1)} %copy-done.8, bf16[128,128]{1,0:T(8,128)(2,1)} %copy-done.33, s32[1,2048]{1,0:T(1,128)} %fusion.1.refs_2_, s32[1,2048]{1,0:T(1,128)} %bitcast.67, ...), custom_call_target="tpu_custom_call" | custom-call | flops 1 | bytes 1 | tf_op jit(solution)/shard_map/attention_forward_backward/pallas_call | solution.py:90
  193.3 7.0 %collective-permute-done.10.refs_6_ = bf16[256,3456]{1,0:T(8,128)(2,1)S(1)} collective-permute-done((bf16[256,3456]{1,0:T(8,128)(2,1)}, bf16[256,3456]{1,0:T(8,128)(2,1)S(1)}, u32[]{:S(2)}, u32[]{:S(2)}) %collective-permute-start.10) | collective-permute-done | bytes 1769504 | tf_op jit(solution)/shard_map/ppermute | solution.py:1320
  201.5 6.5 %own_grads.2 = (bf16[16,192,384]{2,1,0:T(8,128)(2,1)}, f32[8,128]{1,0:T(8,128)}) custom-call(s32[9]{0:T(128)} %stack.39.at, bf16[128,1536]{1,0:T(8,128)(2,1)} %get-tuple-element.134.refs_0_.refs_8_.refs_1_, bf16[128,1536]{1,0:T(8,128)(2,1)} %copy-done.7, bf16[128,768]{1,0:T(8,128)(2,1)} %bitcast.57, bf16[128,768]{1,0:T(8,128)(2,1)} %copy-done.13, ...), custom_call_target="tpu_custom_call" | custom-call | flops 1 | bytes 1 | tf_op jit(solution)/shard_map/own_grads/pallas_call | solution.py:90
  210.4 11.9 %collective-permute-start.12 = (f32[128,768]{1,0:T(8,128)S(1)}, f32[128,768]{1,0:T(8,128)S(1)}, u32[]{:S(2)}, u32[]{:S(2)}) collective-permute-start(f32[128,768]{1,0:T(8,128)S(1)} %copy-done.37), channel_id=1, source_target_pairs={{0,2},{2,0},{1,3},{3,1},{4,6},{6,4},{5,7},{7,5},{8,10},{10,8},{9,1... | collective-permute-start | bytes 1179656 | tf_op jit(solution)/shard_map/ppermute | solution.py:1154
  246.0 7.4 %mlp_back.3 = (bf16[256,1536]{1,0:T(8,128)(2,1)}, f32[128,768]{1,0:T(8,128)}, f32[128,768]{1,0:T(8,128)}, f32[4,384]{1,0:T(4,128)}, bf16[256,2304]{1,0:T(8,128)(2,1)}) custom-call(s32[9]{0:T(128)} %stack.39.at, bf16[128,768]{1,0:T(8,128)(2,1)} %get-tuple-element.161.refs_0_.refs_2_, bf16[128,768]{1,0:T(8,128)(2,1)} %copy-done.16, ...), custom_call_target="tpu_custom_call" | custom-call | flops 1 | bytes 1 | tf_op jit(solution)/shard_map/mlp_back/pallas_call | solution.py:90
  263.9 9.6 %attention_backward.1 = (bf16[16,192,128]{2,1,0:T(8,128)(2,1)}, f32[128,128]{1,0:T(8,128)}, f32[128,128]{1,0:T(8,128)}) custom-call(s32[9]{0:T(128)} %stack.39.at, bf16[16,192,128]{2,1,0:T(8,128)(2,1)} %copy-done.3, bf16[128,128]{1,0:T(8,128)(2,1)} %copy-done.30, s32[1,2048]{1,0:T(1,128)} %fusion.1.refs_2_, s32[1,2048]{1,0:T(1,128)} %bitcast.68, ...), custom_call_target="tpu_custom_call" | custom-call | flops 1 | bytes 1 | tf_op jit(solution)/shard_map/attention_backward/pallas_call | solution.py:90
  281.5 5.5 %all-to-all-start.5 = ((bf16[16,192,128]{2,1,0:T(8,128)(2,1)}), bf16[16,192,128]{2,1,0:T(8,128)(2,1)S(1)}, u32[]{:S(2)}, u32[]{:S(2)}) async-start(bf16[16,192,128]{2,1,0:T(8,128)(2,1)} %attention_edge.3.refs_9_), calls=%async_computation.6 | async-start | bytes 1572864 | tf_op jit(solution)/shard_map/all_to_all | solution.py:1273
  292.0 7.4 %own_grads.3 = (bf16[16,224,384]{2,1,0:T(8,128)(2,1)}, f32[8,128]{1,0:T(8,128)}) custom-call(s32[9]{0:T(128)} %stack.39.at, bf16[128,1536]{1,0:T(8,128)(2,1)} %get-tuple-element.117.refs_0_.refs_1_, bf16[128,1536]{1,0:T(8,128)(2,1)} %copy-done.6, bf16[128,768]{1,0:T(8,128)(2,1)} %get-tuple-element.161.refs_0_.refs_2_, bf16[128,768]{1,0:T(8,128)(2,1)} %copy-done.16, ...), custom_call_target="tpu_custom_call" | custom-call | flops 1 | bytes 1 | tf_op jit(solution)/shard_map/own_grads/pallas_call | solution.py:90
  306.7 7.1 %collective-permute-start.18 = (f32[128,768]{1,0:T(8,128)S(1)}, f32[128,768]{1,0:T(8,128)S(1)}, u32[]{:S(2)}, u32[]{:S(2)}) collective-permute-start(f32[128,768]{1,0:T(8,128)S(1)} %copy-done.36), channel_id=1, source_target_pairs={{0,2},{2,0},{1,3},{3,1},{4,6},{6,4},{5,7},{7,5},{8,10},{10,8},{9,1... | collective-permute-start | bytes 1179656 | tf_op jit(solution)/shard_map/ppermute | solution.py:1154
  325.8 17.1 %all-to-all-done.6 = bf16[16,224,384]{2,1,0:T(8,128)(2,1)S(1)} async-done(((bf16[16,224,384]{2,1,0:T(8,128)(2,1)}), bf16[16,224,384]{2,1,0:T(8,128)(2,1)S(1)}, u32[]{:S(2)}, u32[]{:S(2)}) %all-to-all-start.6) | async-done | bytes 2752544 | tf_op jit(solution)/shard_map/all_to_all | solution.py:1190
  348.4 8.1 %reduce-scatter.11.cloned.1.call-done.refs_1_ = bf16[192,384]{1,0:T(8,128)(2,1)} async-done(((bf16[768,384]{1,0:T(8,128)(2,1)}), bf16[192,384]{1,0:T(8,128)(2,1)}) %reduce-scatter.11.cloned.1.call-update) | async-done | bytes 147472 | tf_op jit(solution)/shard_map/reduce_scatter | solution.py:1186
  374.4 37.5 %all_to_all.45 = bf16[64,40,384]{2,1,0:T(8,128)(2,1)} all-to-all(bf16[64,40,384]{2,1,0:T(8,128)(2,1)S(1)} %bitcast.50), channel_id=1, replica_groups=mesh['xh'=2,'xl'=2,'zl'=2,'y'=4,'core'=2,'zh'=2] {'zh','xh','xl','y','zl'}, dimensions={0} | all-to-all | bytes 3932160 | tf_op jit(solution)/shard_map/all_to_all | solution.py:1159
  413.8 29.7 %all_to_all.46 = bf16[32,40,384]{2,1,0:T(8,128)(2,1)S(1)} all-to-all(bf16[32,40,384]{2,1,0:T(8,128)(2,1)S(1)} %broadcast_in_dim.60), channel_id=1, replica_groups=mesh['xh'=2,'xl'=2,'zl'=2,'y'=4,'core'=2,'zh'=2] {'xh','xl','y','zl'}, dimensions={0} | all-to-all | bytes 1966080 | tf_op jit(solution)/shard_map/all_to_all | solution.py:1211
  452.0 5.7 %place_qkv.1 = (f32[2,384,2304]{2,1,0:T(8,128)}, f32[2,2,384]{2,1,0:T(2,128)}, f32[2,2,384]{2,1,0:T(2,128)}, f32[2,384]{1,0:T(2,128)}, f32[2,384]{1,0:T(2,128)}, /*index=5*/f32[2,1152]{1,0:T(2,128)}, f32[2,1536]{1,0:T(2,128)}) custom-call(s32[9]{0:T(128)} %stack.39.at, bf16[1280,384]{1,0:T(8,128)(2,1)} %bitcast.62, bf16[1280,384]{1,0:T(8,128)(2,1)} %copy-done.21, ...), custom_call_target="tpu_custom_call" | custom-call | flops 1 | bytes 1 | tf_op jit(solution)/shard_map/place_qkv/pallas_call | solution.py:90
  461.4 6.9 %collective-permute-done.24 = f32[128,768]{1,0:T(8,128)S(1)} collective-permute-done((f32[128,768]{1,0:T(8,128)S(1)}, f32[128,768]{1,0:T(8,128)S(1)}, u32[]{:S(2)}, u32[]{:S(2)}) %collective-permute-start.24) | collective-permute-done | bytes 393248 | tf_op jit(solution)/shard_map/ppermute | solution.py:1154
  472.0 16.0 %place_long.1 = (f32[2,384,3072]{2,1,0:T(8,128)}, f32[2,1536,768]{2,1,0:T(8,128)}, f32[2,384,768]{2,1,0:T(8,128)}, f32[2,384,2304]{2,1,0:T(8,128)}) custom-call(s32[9]{0:T(128)} %stack.39.at, bf16[8192,384]{1,0:T(8,128)(2,1)} %get-tuple-element.206.mine_ref, bf16[8192,384]{1,0:T(8,128)(2,1)} %collective-permute-done.26.theirs_ref, ...), custom_call_target="tpu_custom_call", output_to_operand_aliasing={{3}: (3, {})} | custom-call | flops 1 | bytes 1 | tf_op jit(solution)/shard_map/place_long/pallas_call | solution.py:1023
  (223 shorter events, 211.2 us)
Async XLA Ops:
  7.2 98.6 %all-gather.4.cloned.1.call-start = ((), (), s32[]{:S(2)}) async-start(), calls=%async_computation.13 | async-start | bytes 2506752 | tf_op jit(solution)/shard_map/all_gather | solution.py:1286
  12.1 28.2 %collective-permute-start = (bf16[1376,384]{1,0:T(8,128)(2,1)}, bf16[1376,384]{1,0:T(8,128)(2,1)S(1)}, u32[]{:S(2)}, u32[]{:S(2)}) collective-permute-start(bf16[1376,384]{1,0:T(8,128)(2,1)} %begin.1.refs_0_.refs_2_.refs_1_), channel_id=1, source_target_pairs={{0,1},{1,0},{2,3},{3,2},{4,5},{5,4},{6,7},{7,6},{8,9},{9,8},{10,11... | collective-permute-start | bytes 3170312 | tf_op jit(solution)/shard_map/ppermute | solution.py:1289
  53.8 19.6 %all-to-all-start = ((bf16[16,192,128]{2,1,0:T(8,128)(2,1)}), bf16[16,192,128]{2,1,0:T(8,128)(2,1)S(1)}, u32[]{:S(2)}, u32[]{:S(2)}) async-start(bf16[16,192,128]{2,1,0:T(8,128)(2,1)} %bitcast.54), calls=%async_computation | async-start | bytes 1572864 | tf_op jit(solution)/shard_map/all_to_all | solution.py:1273
  59.7 82.0 %all-gather.6.cloned.1.call-start = ((), (), s32[]{:S(2)}) async-start(), calls=%async_computation.14 | async-start | bytes 2506752 | tf_op jit(solution)/shard_map/all_gather | solution.py:1286
  75.7 19.1 %collective-permute-start.3 = (bf16[960,384]{1,0:T(8,128)(2,1)}, bf16[960,384]{1,0:T(8,128)(2,1)S(1)}, u32[]{:S(2)}, u32[]{:S(2)}) collective-permute-start(bf16[960,384]{1,0:T(8,128)(2,1)} %get-tuple-element.124), channel_id=1, source_target_pairs={{0,1},{1,0},{2,3},{3,2},{4,5},{5,4},{6,7},{7,6},{8,9},{9,8},{10,11... | collective-permute-start | bytes 2211848 | tf_op jit(solution)/shard_map/ppermute | solution.py:1299
  96.8 19.7 %all-to-all-start.1 = ((bf16[16,64,128]{2,1,0:T(8,128)(2,1)}), bf16[16,64,128]{2,1,0:T(8,128)(2,1)S(1)}, u32[]{:S(2)}, u32[]{:S(2)}) async-start(bf16[16,64,128]{2,1,0:T(8,128)(2,1)} %get-tuple-element.123), calls=%async_computation.1 | async-start | bytes 524288 | tf_op jit(solution)/shard_map/all_to_all | solution.py:1273
  100.4 12.5 %collective-permute-start.4 = (bf16[128,768]{1,0:T(8,128)(2,1)S(1)}, bf16[128,768]{1,0:T(8,128)(2,1)S(1)}, u32[]{:S(2)}, u32[]{:S(2)}) collective-permute-start(bf16[128,768]{1,0:T(8,128)(2,1)S(1)} %bitcast.60), channel_id=1, source_target_pairs={{0,2},{2,0},{1,3},{3,1},{4,6},{6,4},{5,7},{7,5},{8,10},{10,8},{9,1... | collective-permute-start | bytes 589832 | tf_op jit(solution)/shard_map/ppermute | solution.py:1154
  102.8 25.2 %collective-permute-start.7 = (bf16[1152,384]{1,0:T(8,128)(2,1)}, bf16[1152,384]{1,0:T(8,128)(2,1)S(1)}, u32[]{:S(2)}, u32[]{:S(2)}) collective-permute-start(bf16[1152,384]{1,0:T(8,128)(2,1)} %get-tuple-element.135.refs_2_.refs_1_), channel_id=1, source_target_pairs={{0,1},{1,0},{2,3},{3,2},{4,5},{5,4},{6,7},{7,6},{8,9},{9,8},{10,11... | collective-permute-start | bytes 2654216 | tf_op jit(solution)/shard_map/ppermute | solution.py:1301
  133.4 23.1 %all-to-all-start.2 = ((bf16[16,256,128]{2,1,0:T(8,128)(2,1)}), bf16[16,256,128]{2,1,0:T(8,128)(2,1)S(1)}, u32[]{:S(2)}, u32[]{:S(2)}) async-start(bf16[16,256,128]{2,1,0:T(8,128)(2,1)} %bitcast.53), calls=%async_computation.2 | async-start | bytes 2097152 | tf_op jit(solution)/shard_map/all_to_all | solution.py:1273
  158.8 41.5 %collective-permute-start.10 = (bf16[256,3456]{1,0:T(8,128)(2,1)}, bf16[256,3456]{1,0:T(8,128)(2,1)S(1)}, u32[]{:S(2)}, u32[]{:S(2)}) collective-permute-start(bf16[256,3456]{1,0:T(8,128)(2,1)} %get-tuple-element.150), channel_id=1, source_target_pairs={{0,1},{1,0},{2,3},{3,2},{4,5},{5,4},{6,7},{7,6},{8,9},{9,8},{10,11... | collective-permute-start | bytes 5308424 | tf_op jit(solution)/shard_map/ppermute | solution.py:1320
  189.4 18.6 %all-to-all-start.3 = ((bf16[16,256,128]{2,1,0:T(8,128)(2,1)}), bf16[16,256,128]{2,1,0:T(8,128)(2,1)S(1)}, u32[]{:S(2)}, u32[]{:S(2)}) async-start(bf16[16,256,128]{2,1,0:T(8,128)(2,1)} %attention_edge.2.refs_7_), calls=%async_computation.3 | async-start | bytes 2097152 | tf_op jit(solution)/shard_map/all_to_all | solution.py:1273
  193.0 65.8 %reduce-scatter.5.cloned.1.call-start = ((), (), s32[]{:S(2)}) async-start(), calls=%async_computation.15 | async-start | bytes 2949120 | tf_op jit(solution)/shard_map/reduce_scatter | solution.py:1182
  210.4 22.0 %collective-permute-start.12 = (f32[128,768]{1,0:T(8,128)S(1)}, f32[128,768]{1,0:T(8,128)S(1)}, u32[]{:S(2)}, u32[]{:S(2)}) collective-permute-start(f32[128,768]{1,0:T(8,128)S(1)} %copy-done.37), channel_id=1, source_target_pairs={{0,2},{2,0},{1,3},{3,1},{4,6},{6,4},{5,7},{7,5},{8,10},{10,8},{9,1... | collective-permute-start | bytes 1179656 | tf_op jit(solution)/shard_map/ppermute | solution.py:1154
  229.5 29.2 %collective-permute-start.14 = (bf16[256,1408]{1,0:T(8,128)(2,1)}, bf16[256,1408]{1,0:T(8,128)(2,1)S(1)}, u32[]{:S(2)}, u32[]{:S(2)}) collective-permute-start(bf16[256,1408]{1,0:T(8,128)(2,1)} %pack_early.1.refs_8_), channel_id=1, source_target_pairs={{0,1},{1,0},{2,3},{3,2},{4,5},{5,4},{6,7},{7,6},{8,9},{9,8},{10,11... | collective-permute-start | bytes 2162696 | tf_op jit(solution)/shard_map/ppermute | solution.py:1328
  242.4 16.4 %all-to-all-start.4 = ((bf16[16,64,128]{2,1,0:T(8,128)(2,1)}), bf16[16,64,128]{2,1,0:T(8,128)(2,1)S(1)}, u32[]{:S(2)}, u32[]{:S(2)}) async-start(bf16[16,64,128]{2,1,0:T(8,128)(2,1)} %grad_ctx.3.refs_8_), calls=%async_computation.4 | async-start | bytes 524288 | tf_op jit(solution)/shard_map/all_to_all | solution.py:1273
  246.0 78.2 %reduce-scatter.9.cloned.1.call-start = ((), (), s32[]{:S(2)}) async-start(), calls=%async_computation.17 | async-start | bytes 737280 | tf_op jit(solution)/shard_map/reduce_scatter | solution.py:1186
  261.0 63.2 %reduce-scatter.7.cloned.1.call-start = ((), (), s32[]{:S(2)}) async-start(), calls=%async_computation.16 | async-start | bytes 2949120 | tf_op jit(solution)/shard_map/reduce_scatter | solution.py:1182
  262.2 28.7 %collective-permute-start.16 = (bf16[256,2304]{1,0:T(8,128)(2,1)S(1)}, bf16[256,2304]{1,0:T(8,128)(2,1)S(1)}, u32[]{:S(2)}, u32[]{:S(2)}) collective-permute-start(bf16[256,2304]{1,0:T(8,128)(2,1)S(1)} %copy-done.20), channel_id=1, source_target_pairs={{0,1},{1,0},{2,3},{3,2},{4,5},{5,4},{6,7},{7,6},{8,9},{9,8},{10,11... | collective-permute-start | bytes 3538952 | tf_op jit(solution)/shard_map/ppermute | solution.py:1337
  281.5 17.8 %all-to-all-start.5 = ((bf16[16,192,128]{2,1,0:T(8,128)(2,1)}), bf16[16,192,128]{2,1,0:T(8,128)(2,1)S(1)}, u32[]{:S(2)}, u32[]{:S(2)}) async-start(bf16[16,192,128]{2,1,0:T(8,128)(2,1)} %attention_edge.3.refs_9_), calls=%async_computation.6 | async-start | bytes 1572864 | tf_op jit(solution)/shard_map/all_to_all | solution.py:1273
  301.5 41.4 %all-to-all-start.6 = ((bf16[16,224,384]{2,1,0:T(8,128)(2,1)}), bf16[16,224,384]{2,1,0:T(8,128)(2,1)S(1)}, u32[]{:S(2)}, u32[]{:S(2)}) async-start(bf16[16,224,384]{2,1,0:T(8,128)(2,1)} %get-tuple-element.187), calls=%async_computation.7 | async-start | bytes 5505024 | tf_op jit(solution)/shard_map/all_to_all | solution.py:1190
  306.7 49.8 %reduce-scatter.11.cloned.1.call-start = ((), (), s32[]{:S(2)}) async-start(), calls=%async_computation.18 | async-start | bytes 737280 | tf_op jit(solution)/shard_map/reduce_scatter | solution.py:1186
  306.7 11.4 %collective-permute-start.18 = (f32[128,768]{1,0:T(8,128)S(1)}, f32[128,768]{1,0:T(8,128)S(1)}, u32[]{:S(2)}, u32[]{:S(2)}) collective-permute-start(f32[128,768]{1,0:T(8,128)S(1)} %copy-done.36), channel_id=1, source_target_pairs={{0,2},{2,0},{1,3},{3,1},{4,6},{6,4},{5,7},{7,5},{8,10},{10,8},{9,1... | collective-permute-start | bytes 1179656 | tf_op jit(solution)/shard_map/ppermute | solution.py:1154
  325.5 133.8 %all-gather.8.cloned.1.call-start = ((), (), s32[]{:S(2)}) async-start(), calls=%async_computation.19 | async-start | bytes 6684672 | tf_op jit(solution)/shard_map/all_gather | solution.py:1356
  460.7 11.4 %collective-permute-start.26 = (bf16[8192,384]{1,0:T(8,128)(2,1)}, bf16[8192,384]{1,0:T(8,128)(2,1)}, u32[]{:S(2)}, u32[]{:S(2)}) collective-permute-start(bf16[8192,384]{1,0:T(8,128)(2,1)} %get-tuple-element.206.mine_ref), channel_id=1, source_target_pairs={{0,2},{2,0},{1,3},{3,1},{4,6},{6,4},{5,7},{7,5},{8,10},{10,8},{9,1... | collective-permute-start | bytes 18874376 | tf_op jit(solution)/shard_map/ppermute | solution.py:1154
  (56 other events, 272.6 us)
Sparse Core Ops, SparseCore 0:
  41.1 50.6 all-gather.3
  96.9 44.6 all-gather.5
  210.5 42.2 reduce-scatter.4
  261.1 19.7 reduce-scatter.8
  283.8 39.5 reduce-scatter.6
  325.6 30.8 reduce-scatter.10
  374.5 84.7 all-gather.7
